TPU v7x, 32 devices: a whole 2x2x4 slice. The times are simulated.
32 devices in a mesh: groups: 1, gx: 4 (over z), gy: 4 (over y, x), gz: 2 (over core).
Axes of the slice: x: 2, y: 2, z: 4, core: 2. Of those that a mesh axis runs over, the one named last changes fastest.
Arguments:
- modes: float32 [3, 16, 32, 8, 128], P('groups', 'gx', 'gy', 'gz'), may hold values from -6 to 6
- cell_weight: float32 [16, 32, 8], P('gx', 'gy', 'gz'), may hold values from 0.25 to 4
- pair_owner: int32 [32], replicated, may hold values from 0 to 31, each once
Outputs:
- convective: float32 [64, 8256], P('groups', ('gx', 'gy', 'gz'))
All inputs are finite; a program needn't handle non-finite values.
Results may differ from a plain program's by a relative error of at most 0.000098.
Values sent between devices are 32-bit elements; how exact they have to be, the bound alone decides.
A program may use at most 64 MiB of HBM per device.

v0:
```python
import jax
import jax.numpy as jnp
import numpy as np
from jax import lax
from jax.sharding import PartitionSpec as P

TEST = 64


def extended(value, sides, width):
    for axis, dim in sides:
        peers, length = (lax.axis_size(axis), value.shape[dim])
        up = [(i, (i + 1) % peers) for i in range(peers)]
        down = [(j, i) for i, j in up]
        last = lax.slice_in_dim(value, length - width, length, axis=dim)
        leading = lax.slice_in_dim(value, 0, width, axis=dim)
        before = lax.ppermute(last, axis, up)
        after = lax.ppermute(leading, axis, down)
        value = jnp.concatenate([before, value, after], axis=dim)
    return value


def gradients(padded):
    step_x = (padded[:, 2:, 1:-1, 1:-1] - padded[:, :-2, 1:-1, 1:-1]) * 0.5
    step_y = (padded[:, 1:-1, 2:, 1:-1] - padded[:, 1:-1, :-2, 1:-1]) * 0.5
    step_z = (padded[:, 1:-1, 1:-1, 2:] - padded[:, 1:-1, 1:-1, :-2]) * 0.5
    return jnp.stack([step_x, step_y, step_z], axis=1)


def assemble(mode_flat, grad_flat, weight_flat, test_count, block_size):
    weighted = mode_flat[:, :, :test_count] * weight_flat[None, :, None]
    cells = weighted.shape[1]
    blocks = weighted.reshape(3, cells, test_count // block_size, block_size).transpose(2, 0, 1, 3)

    def one_block(chosen):
        zeta = jnp.einsum("axi,abxk->ibxk", chosen, grad_flat, precision=lax.Precision.HIGHEST)
        return jnp.einsum("ibxk,bxj->ijk", zeta, mode_flat, precision=lax.Precision.HIGHEST)

    result = lax.map(one_block, blocks)
    width = mode_flat.shape[2]
    return result.reshape(test_count, width, width)


def shards(modes, cell_weight, pair_owner):
    width = modes.shape[4]
    size_x = lax.axis_size("gx")
    size_y = lax.axis_size("gy")
    size_z = lax.axis_size("gz")
    owners = size_x * size_y * size_z
    padded = extended(modes, (("gx", 1), ("gy", 2), ("gz", 3)), 1)
    depth = padded.shape[3]
    layer = lax.broadcasted_iota(jnp.int32, (1, 1, 1, depth, 1), 3)
    level = lax.axis_index("gz")
    outside = (layer == 0) & (level == 0) | (layer == depth - 1) & (level == size_z - 1)
    padded = jnp.where(outside, jnp.float32(0.0), padded)
    grads = gradients(padded)
    mode_flat = modes.reshape(3, -1, width)
    grad_flat = grads.reshape(3, 3, -1, width)
    weight_flat = cell_weight.reshape(-1)
    total_cells = modes.shape[1] * modes.shape[2] * modes.shape[3] * owners
    scale = 1.0 / jnp.sqrt(jnp.float32(3.0 * total_cells))
    tensor = assemble(mode_flat, grad_flat, weight_flat, TEST, 8) * scale
    pair_total = width * (width + 1) // 2
    block_len = (pair_total + owners - 1) // owners
    upper_j, upper_k = np.triu_indices(width)
    table_j = jnp.asarray(upper_j.astype(np.int32))
    table_k = jnp.asarray(upper_k.astype(np.int32))
    slots = jnp.arange(block_len * owners, dtype=jnp.int32)
    position = slots // block_len
    within = slots % block_len
    pair_index = jnp.take(pair_owner, position) * block_len + within
    valid = pair_index < pair_total
    clipped = jnp.minimum(pair_index, pair_total - 1)
    index_j = jnp.take(table_j, clipped)
    index_k = jnp.take(table_k, clipped)
    flattened = tensor.reshape(TEST, width * width)
    summed = jnp.take(flattened, index_j * width + index_k, axis=1) + jnp.take(
        flattened, index_k * width + index_j, axis=1
    )
    partial_terms = jnp.where(valid[None, :], summed, jnp.float32(0.0))
    owned = lax.psum_scatter(partial_terms, ("gx", "gy", "gz"), scatter_dimension=1, tiled=True)
    return owned


def solution(mesh):
    placed = (P("groups", "gx", "gy", "gz", None), P("gx", "gy", "gz"), P())
    return jax.shard_map(
        shards,
        mesh=mesh,
        in_specs=placed,
        out_specs=P("groups", ("gx", "gy", "gz")),
        check_vma=False,
    )
```

profile of v0, /device:TPU:0, one launch (start us, length us, event | category | flops | bytes accessed | tf_op | source)
XLA Modules:
  0.0 340.5 jit_solution(8372125762917601217)
XLA Ops:
  0.0 0.8 fusion.27
  0.8 3.1 collective-permute-start
  3.9 2.1 collective-permute-start.1
  6.0 1.8 fusion.29
  7.8 2.1 fusion.28
  9.9 0.2 compare_reduce_fusion
  10.1 0.2 compare_reduce_fusion.1
  10.3 0.2 compare_reduce_fusion.10
  10.5 0.2 compare_reduce_fusion.11
  10.6 0.2 compare_reduce_fusion.12
  10.8 0.2 compare_reduce_fusion.13
  11.0 0.2 compare_reduce_fusion.14
  11.2 0.2 compare_reduce_fusion.15
  11.4 0.2 compare_reduce_fusion.16
  11.6 0.2 compare_reduce_fusion.17
  11.7 0.2 compare_reduce_fusion.18
  11.9 0.2 compare_reduce_fusion.19
  12.1 0.2 compare_reduce_fusion.2
  12.3 0.2 compare_reduce_fusion.20
  12.8 0.2 compare_reduce_fusion.23
  13.2 0.2 compare_reduce_fusion.3
  14.1 0.2 compare_reduce_fusion.8
  14.5 4.6 %fusion.24 = s32[8256]{0:T(1024)S(1)} fusion(s32[]{:T(128)} %bitcast.34, s32[]{:T(128)} %bitcast.35, s32[]{:T(128)} %bitcast.36, s32[]{:T(128)} %bitcast.37, s32[]{:T(128)} %bitcast.38, s32[]{:T(128)} %bitcast.40, s32[]{:T(128)} %bitcast.39), kind=kLoop, calls=%fused_computation.88 | loop fusion | flops 189888 | bytes 33052 | tf_op jit(solution)/shard_map/jit(_take)/gather | solution.py:71
  19.1 15.8 %broadcast_compare_fusion = (pred[8256]{0:T(1024)(128)(4,1)S(1)}, s32[8256]{0:T(1024)S(1)}) fusion(pred[8256]{0:T(1024)(128)(4,1)S(1)} %compare_reduce_fusion, pred[8256]{0:T(1024)(128)(4,1)S(1)} %compare_reduce_fusion.1, pred[8256]{0:T(1024)(128)(4,1)S(1)} %compare_reduce_fusion.2, pred[8256]{0:T(1024)(128)(4,1)S(1)} %compare_reduce_fusion.3, ...), kind=kLoop, calls=%fused_computation.89 | loop fusion | flops 388032 | bytes 280804 | tf_op jit(solution)/shard_map/lt | solution.py:72
  35.0 42.8 %gather_fusion = s32[8256]{0:T(1024)S(1)} fusion(s32[8256]{0:T(1024)S(1)} %copy-done, s32[9216]{0:T(1024)S(1)} %pad_clamp_fusion.2), kind=kCustom, calls=%fused_computation.clone | custom fusion | bytes 99072 | tf_op jit(solution)/shard_map/jit(_take)/gather | solution.py:74
  77.8 42.8 %gather_fusion.1 = s32[8256]{0:T(1024)S(1)} fusion(s32[8256]{0:T(1024)S(1)} %copy-done.1, s32[9216]{0:T(1024)S(1)} %pad_clamp_fusion.2), kind=kCustom, calls=%fused_computation.2.clone | custom fusion | bytes 99072 | tf_op jit(solution)/shard_map/jit(_take)/gather | solution.py:75
  121.2 1.7 collective-permute-start.2
  122.9 1.3 collective-permute-start.3
  124.2 2.1 collective-permute-done.2
  126.3 0.5 collective-permute-done.3
  127.1 0.5 collective-permute-start.5
  127.6 0.8 collective-permute-done.4
  128.5 0.3 maximum_select_fusion
  128.8 0.2 fusion.14
  129.6 47.1 %while.10 = (s32[]{:T(128)}, f32[8,8,128,128]{2,3,1,0:T(8,128)}, f32[8,3,128,8]{2,3,0,1:T(8,128)S(1)}, f32[3,3,128,128]{3,0,1,2:T(4,128)S(1)}, f32[3,128,128]{2,1,0:T(8,128)S(1)}, /*index=5*/s32[]{:T(128)}) while((s32[]{:T(128)}, f32[8,8,128,128]{2,3,1,0:T(8,128)}, f32[8,3,128,8]{2,3,0,1:T(8,128)S(1)}, f32[3,3,128,128]{3,0,1,2:T(4,128)S(1)}, ...), condition=%wide.region_1.2_spmd, body=%wide.region_0.1_spmd.sunk | while | flops 618135552 | bytes 4518473 | solution.py:39
  129.8 2.2 convolution_bitcast_fusion.2
  132.0 3.5 %fusion.40 = f32[8,8,128,128]{2,3,1,0:T(8,128)} fusion(f32[8,8,128,128]{2,3,1,0:T(8,128)} %get-tuple-element.151, s32[]{:T(128)} %get-tuple-element.150, f32[8,3,128,128]{3,0,1,2:T(8,128)S(1)} %convolution_bitcast_fusion.2, f32[3,128,128]{2,1,0:T(8,128)S(1)} %get-tuple-element.160), kind=kOutput, calls=%fused_computation.8.clone.1 | convolution fusion | flops 603979776 | bytes 2294272 | tf_op jit(solution)/shard_map/while/body/eval_jaxpr/ibxk,bxj->ijk/dot_general | solution.py:37
  135.6 2.2 convolution_bitcast_fusion.2
  137.8 3.5 %fusion.40 = f32[8,8,128,128]{2,3,1,0:T(8,128)} fusion(f32[8,8,128,128]{2,3,1,0:T(8,128)} %get-tuple-element.151, s32[]{:T(128)} %get-tuple-element.150, f32[8,3,128,128]{3,0,1,2:T(8,128)S(1)} %convolution_bitcast_fusion.2, f32[3,128,128]{2,1,0:T(8,128)S(1)} %get-tuple-element.160), kind=kOutput, calls=%fused_computation.8.clone.1 | convolution fusion | flops 603979776 | bytes 2294272 | tf_op jit(solution)/shard_map/while/body/eval_jaxpr/ibxk,bxj->ijk/dot_general | solution.py:37
  141.5 2.2 convolution_bitcast_fusion.2
  143.7 3.5 %fusion.40 = f32[8,8,128,128]{2,3,1,0:T(8,128)} fusion(f32[8,8,128,128]{2,3,1,0:T(8,128)} %get-tuple-element.151, s32[]{:T(128)} %get-tuple-element.150, f32[8,3,128,128]{3,0,1,2:T(8,128)S(1)} %convolution_bitcast_fusion.2, f32[3,128,128]{2,1,0:T(8,128)S(1)} %get-tuple-element.160), kind=kOutput, calls=%fused_computation.8.clone.1 | convolution fusion | flops 603979776 | bytes 2294272 | tf_op jit(solution)/shard_map/while/body/eval_jaxpr/ibxk,bxj->ijk/dot_general | solution.py:37
  147.4 2.2 convolution_bitcast_fusion.2
  149.6 3.5 %fusion.40 = f32[8,8,128,128]{2,3,1,0:T(8,128)} fusion(f32[8,8,128,128]{2,3,1,0:T(8,128)} %get-tuple-element.151, s32[]{:T(128)} %get-tuple-element.150, f32[8,3,128,128]{3,0,1,2:T(8,128)S(1)} %convolution_bitcast_fusion.2, f32[3,128,128]{2,1,0:T(8,128)S(1)} %get-tuple-element.160), kind=kOutput, calls=%fused_computation.8.clone.1 | convolution fusion | flops 603979776 | bytes 2294272 | tf_op jit(solution)/shard_map/while/body/eval_jaxpr/ibxk,bxj->ijk/dot_general | solution.py:37
  153.3 2.2 convolution_bitcast_fusion.2
  155.5 3.5 %fusion.40 = f32[8,8,128,128]{2,3,1,0:T(8,128)} fusion(f32[8,8,128,128]{2,3,1,0:T(8,128)} %get-tuple-element.151, s32[]{:T(128)} %get-tuple-element.150, f32[8,3,128,128]{3,0,1,2:T(8,128)S(1)} %convolution_bitcast_fusion.2, f32[3,128,128]{2,1,0:T(8,128)S(1)} %get-tuple-element.160), kind=kOutput, calls=%fused_computation.8.clone.1 | convolution fusion | flops 603979776 | bytes 2294272 | tf_op jit(solution)/shard_map/while/body/eval_jaxpr/ibxk,bxj->ijk/dot_general | solution.py:37
  159.2 2.2 convolution_bitcast_fusion.2
  161.4 3.5 %fusion.40 = f32[8,8,128,128]{2,3,1,0:T(8,128)} fusion(f32[8,8,128,128]{2,3,1,0:T(8,128)} %get-tuple-element.151, s32[]{:T(128)} %get-tuple-element.150, f32[8,3,128,128]{3,0,1,2:T(8,128)S(1)} %convolution_bitcast_fusion.2, f32[3,128,128]{2,1,0:T(8,128)S(1)} %get-tuple-element.160), kind=kOutput, calls=%fused_computation.8.clone.1 | convolution fusion | flops 603979776 | bytes 2294272 | tf_op jit(solution)/shard_map/while/body/eval_jaxpr/ibxk,bxj->ijk/dot_general | solution.py:37
  165.1 2.2 convolution_bitcast_fusion.2
  167.3 3.5 %fusion.40 = f32[8,8,128,128]{2,3,1,0:T(8,128)} fusion(f32[8,8,128,128]{2,3,1,0:T(8,128)} %get-tuple-element.151, s32[]{:T(128)} %get-tuple-element.150, f32[8,3,128,128]{3,0,1,2:T(8,128)S(1)} %convolution_bitcast_fusion.2, f32[3,128,128]{2,1,0:T(8,128)S(1)} %get-tuple-element.160), kind=kOutput, calls=%fused_computation.8.clone.1 | convolution fusion | flops 603979776 | bytes 2294272 | tf_op jit(solution)/shard_map/while/body/eval_jaxpr/ibxk,bxj->ijk/dot_general | solution.py:37
  171.0 2.2 convolution_bitcast_fusion.2
  173.2 3.5 %fusion.40 = f32[8,8,128,128]{2,3,1,0:T(8,128)} fusion(f32[8,8,128,128]{2,3,1,0:T(8,128)} %get-tuple-element.151, s32[]{:T(128)} %get-tuple-element.150, f32[8,3,128,128]{3,0,1,2:T(8,128)S(1)} %convolution_bitcast_fusion.2, f32[3,128,128]{2,1,0:T(8,128)S(1)} %get-tuple-element.160), kind=kOutput, calls=%fused_computation.8.clone.1 | convolution fusion | flops 603979776 | bytes 2294272 | tf_op jit(solution)/shard_map/while/body/eval_jaxpr/ibxk,bxj->ijk/dot_general | solution.py:37
  176.7 4.9 %broadcast_multiply_fusion = f32[8,8,128,128]{2,3,1,0:T(8,128)} fusion(f32[8,8,128,128]{2,3,1,0:T(8,128)} %get-tuple-element.34), kind=kLoop, calls=%fused_computation.15 | loop fusion | flops 1048576 | bytes 8388608 | tf_op jit(solution)/shard_map/mul | solution.py:62
  181.6 5.3 %copy.47 = f32[8,8,128,128]{3,2,1,0:T(8,128)} copy(f32[8,8,128,128]{2,3,1,0:T(8,128)} %broadcast_multiply_fusion) | data formatting | bytes 8388608 | tf_op jit(solution)/shard_map/mul | solution.py:62
  186.9 6.5 %copy.63 = f32[8,8,128,128]{3,1,2,0:T(8,128)} copy(f32[8,8,128,128]{3,2,1,0:T(8,128)} %copy.47) | data formatting | bytes 8388608
  193.5 6.9 %copy.48 = f32[64,16384]{0,1:T(8,128)} copy(f32[64,16384]{1,0:T(8,128)} %bitcast.83) | data formatting | bytes 8388608 | tf_op jit(solution)/shard_map/mul | solution.py:62
  200.4 19.6 %gather_fusion.2 = f32[8256,64]{1,0:T(8,128)} fusion(f32[64,16384]{0,1:T(8,128)} %copy.48, s32[9216]{0:T(1024)S(1)} %pad_clamp_fusion.1), kind=kCustom, calls=%fused_computation.1.clone | custom fusion | bytes 4260096 | tf_op jit(solution)/shard_map/jit(_take)/gather | solution.py:77
  220.0 19.7 %gather_fusion.3 = f32[8256,64]{1,0:T(8,128)} fusion(f32[64,16384]{0,1:T(8,128)} %copy.48, s32[9216]{0:T(1024)S(1)} %pad_clamp_fusion), kind=kCustom, calls=%fused_computation.3.clone | custom fusion | bytes 4260096 | tf_op jit(solution)/shard_map/jit(_take)/gather | solution.py:77
  239.6 12.0 %fusion.11 = f32[64,8256]{0,1:T(8,128)} fusion(f32[8256,64]{1,0:T(8,128)} %gather_fusion.3, f32[8256,64]{1,0:T(8,128)} %gather_fusion.2, pred[8256]{0:T(1024)(128)(4,1)S(1)} %get-tuple-element.70, pred[8256]{0:T(1024)(128)(4,1)S(1)} %get-tuple-element.67, pred[8256]{0:T(1024)(128)(4,1)S(1)} %get-tuple-element.65), kind=kLoop, calls=%fused_computation.13 | loop fusion | flops 2113536 | bytes 6365376 | tf_op jit(solution)/shard_map/jit(_where)/select_n | solution.py:80
  251.7 82.5 %fusion = f32[64,272]{0,1:T(8,128)S(1)} fusion(f32[64,8256]{0,1:T(8,128)} %fusion.11), kind=kCustom, calls=%all-reduce-scatter | all-reduce-scatter fusion | flops 557057 | bytes 2183168
  334.2 1.3 collective-permute-start.6
  335.6 1.3 collective-permute-start.7
  336.9 2.1 collective-permute-done.7
  338.9 0.8 concatenate.13
  339.7 0.8 copy.50
  (60 shorter events, 4.2 us)
Async XLA Ops:
  0.0 35.0 %copy-start = (s32[8256]{0:T(1024)S(1)}, s32[8256]{0:T(1024)}, u32[]{:S(2)}) copy-start(s32[8256]{0:T(1024)} %constant.91.clone2.1) | copy-start | bytes 99076
  0.8 120.2 %collective-permute-start = (f32[3,1,8,4,128]{4,3,2,1,0:T(4,128)S(1)}, f32[3,1,8,4,128]{4,3,2,1,0:T(4,128)S(1)}, u32[]{:S(2)}, u32[]{:S(2)}) collective-permute-start(f32[3,1,8,4,128]{4,3,2,1,0:T(4,128)S(1)} %get-tuple-element.80), channel_id=1, source_target_pairs={{0,8},{8,16},{16,24},{24,0},{1,9},{9,17},{17,25},{25,1},{2,10},{10... | collective-permute-start | bytes 147464 | tf_op jit(solution)/shard_map/ppermute | solution.py:17
  3.9 117.2 %collective-permute-start.1 = (f32[3,1,8,4,128]{4,3,2,1,0:T(4,128)S(1)}, f32[3,1,8,4,128]{4,3,2,1,0:T(4,128)S(1)}, u32[]{:S(2)}, u32[]{:S(2)}) collective-permute-start(f32[3,1,8,4,128]{4,3,2,1,0:T(4,128)S(1)} %get-tuple-element.79), channel_id=1, source_target_pairs={{8,0},{16,8},{24,16},{0,24},{9,1},{17,9},{25,17},{1,25},{10,2},{18... | collective-permute-start | bytes 147464 | tf_op jit(solution)/shard_map/ppermute | solution.py:18
  35.0 42.8 %copy-start.1 = (s32[8256]{0:T(1024)S(1)}, s32[8256]{0:T(1024)}, u32[]{:S(2)}) copy-start(s32[8256]{0:T(1024)} %constant.92.clone2.1) | copy-start | bytes 99076
  77.8 42.8 %copy-start.2 = (f32[3,4,8,4,128]{4,3,2,1,0:T(4,128)S(1)}, f32[3,4,8,4,128]{4,3,2,1,0:T(4,128)}, u32[]{:S(2)}) copy-start(f32[3,4,8,4,128]{4,3,2,1,0:T(4,128)} %param.11) | copy-start | bytes 589828
  77.8 42.9 %copy-start.3 = (f32[4,8,4]{1,2,0:T(4,128)S(1)}, f32[4,8,4]{1,2,0:T(4,128)}, u32[]{:S(2)}) copy-start(f32[4,8,4]{1,2,0:T(4,128)} %param.12) | copy-start | bytes 1540
  121.2 5.2 %collective-permute-start.2 = (f32[3,6,1,4,128]{4,3,2,1,0:T(4,128)S(1)}, f32[3,6,1,4,128]{4,3,2,1,0:T(4,128)S(1)}, u32[]{:S(2)}, u32[]{:S(2)}) collective-permute-start(f32[3,6,1,4,128]{4,3,2,1,0:T(4,128)S(1)} %get-tuple-element.77), channel_id=1, source_target_pairs={{0,2},{2,4},{4,6},{6,0},{1,3},{3,5},{5,7},{7,1},{8,10},{10,12},{12... | collective-permute-start | bytes 110600 | tf_op jit(solution)/shard_map/ppermute | solution.py:17
  122.9 4.0 %collective-permute-start.3 = (f32[3,6,1,4,128]{4,3,2,1,0:T(4,128)S(1)}, f32[3,6,1,4,128]{4,3,2,1,0:T(4,128)S(1)}, u32[]{:S(2)}, u32[]{:S(2)}) collective-permute-start(f32[3,6,1,4,128]{4,3,2,1,0:T(4,128)S(1)} %get-tuple-element.78), channel_id=1, source_target_pairs={{2,0},{4,2},{6,4},{0,6},{3,1},{5,3},{7,5},{1,7},{10,8},{12,10},{14... | collective-permute-start | bytes 110600 | tf_op jit(solution)/shard_map/ppermute | solution.py:18
  127.0 1.4 collective-permute-start.4
  127.1 1.4 collective-permute-start.5
  334.2 4.7 %collective-permute-start.6 = (f32[64,272]{0,1:T(8,128)S(1)}, f32[64,272]{0,1:T(8,128)S(1)}, u32[]{:S(2)}, u32[]{:S(2)}) collective-permute-start(f32[64,272]{0,1:T(8,128)S(1)} %fusion), channel_id=1, source_target_pairs={{0,1},{1,2},{2,3},{3,4},{4,5},{5,6},{6,7},{7,8},{8,9},{9,10},{10,1... | collective-permute-start | bytes 208904
  335.6 3.4 collective-permute-start.7
where the time goes:
time: 342 us; the launch traced here: 340 us
  local copies, waits for them, and re-layouts  152 us (44%)
  blocking collectives  82.5 us (24%)
  matrix products  45.8 us (13%)
  other arithmetic  42.8 us (13%)
  starting transfers between devices  11.3 us (3%)
  waiting for transfers between devices  5.65 us (2%)
    unnamed x1, blocking collectives  82.5 us
    gather x1, local copies, waits for them, and re-layouts, shards(): index_j = jnp.take(table_j, clipped)  42.8 us
    gather x1, local copies, waits for them, and re-layouts, shards(): index_k = jnp.take(table_k, clipped)  42.8 us
    dot_general x8, matrix products, one_block(): jnp.einsum('ibxk,bxj->ijk', zeta, mode_flat, precision=lax.Precision.HIGH...  28.2 us
    gather x1, local copies, waits for them, and re-layouts, shards(): jnp.take(flattened, index_k * width + index_j, axis=1)  19.7 us
    gather x1, local copies, waits for them, and re-layouts, shards(): jnp.take(flattened, index_j * width + index_k, axis=1)  19.6 us
    dot_general x8, matrix products, one_block(): jnp.einsum('axi,abxk->ibxk', chosen, grad_flat, precision=lax.Precision.H...  17.6 us
    lt x1, other arithmetic, shards(): valid = pair_index < pair_total  15.8 us
  transfers between devices with their start and end apart: 8, of which 5 were waited for; matrix products, arithmetic and copies ran while one was open for 34% of the time, Pallas kernels for 0%

commit v1 on v0

v1 whole, which is shorter than its diff:
```python
import functools
import math
import jax
import jax.numpy as jnp
from jax import lax
from jax.experimental import pallas as pl
from jax.experimental.pallas import tpu as pltpu
from jax.sharding import PartitionSpec as P

TEST = 64
LANES = 128
CHUNK = 688


def halo(value, axis, dim, periodic):
    peers, length = lax.axis_size(axis), value.shape[dim]
    up = [(i, (i + 1) % peers) for i in range(peers if periodic else peers - 1)]
    down = [(j, i) for i, j in up]
    last = lax.slice_in_dim(value, length - 1, length, axis=dim)
    leading = lax.slice_in_dim(value, 0, 1, axis=dim)
    return lax.ppermute(last, axis, up), lax.ppermute(leading, axis, down)


def gradient_tables(nx, ny, nz, m_ref, xb, xa, yb, ya, zb, za, mt, gt, ext, eyt, ezt):
    cells = nx * ny * nz
    plane = ny * nz
    width = m_ref.shape[-1]
    for a in range(3):
        m = m_ref[a]
        mt[a, pl.ds(0, width), :] = m.T
        mt[a, pl.ds(width, 8), :] = jnp.zeros((8, cells), jnp.float32)
        ext[pl.ds(0, plane), :] = xb[a]
        ext[pl.ds(plane, cells), :] = m
        ext[pl.ds(plane + cells, plane), :] = xa[a]
        step = (ext[pl.ds(2 * plane, cells), :] - ext[pl.ds(0, cells), :]) * 0.5
        gt[3 * a, pl.ds(0, width), :] = step.T
        for x in range(nx):
            eyt[x, pl.ds(0, nz), :] = yb[a, pl.ds(x * nz, nz), :]
            eyt[x, pl.ds(nz, plane), :] = m[x * plane:(x + 1) * plane]
            eyt[x, pl.ds(nz + plane, nz), :] = ya[a, pl.ds(x * nz, nz), :]
        step = (eyt[:, pl.ds(2 * nz, plane), :] - eyt[:, pl.ds(0, plane), :]) * 0.5
        gt[3 * a + 1, pl.ds(0, width), :] = step.reshape(cells, width).T
        ezt[0, pl.ds(8, cells), :] = m
        ezt[1, pl.ds(0, cells), :] = ezt[0, pl.ds(9, cells), :]
        ezt[0, pl.ds(0, cells), :] = ezt[0, pl.ds(7, cells), :]
        ezt[0, pl.ds(0, nx * ny, stride=nz), :] = zb[a]
        ezt[1, pl.ds(nz - 1, nx * ny, stride=nz), :] = za[a]
        step = (ezt[1, pl.ds(0, cells), :] - ezt[0, pl.ds(0, cells), :]) * 0.5
        gt[3 * a + 2, pl.ds(0, width), :] = step.T
        for b in range(3):
            gt[3 * a + b, pl.ds(width, 8), :] = jnp.zeros((8, cells), jnp.float32)


def pair_products(width, mt, gt, hbuf):
    for group in range(width // 8):
        tiles = width // 8 - group

        @pl.loop(group * 8, group * 8 + 8)
        def _(j):
            start = j * width - (j * (j - 1)) // 2
            mj = [mt[b, pl.ds(j, 1), :] for b in range(3)]
            gj = [gt[c, pl.ds(j, 1), :] for c in range(9)]
            for t in range(tiles):
                mk = [mt[b, pl.ds(j + 8 * t, 8), :] for b in range(3)]
                for a in range(3):
                    terms = [
                        mj[b] * gt[3 * a + b, pl.ds(j + 8 * t, 8), :] + gj[3 * a + b] * mk[b]
                        for b in range(3)
                    ]
                    hbuf[a, pl.ds(start + 8 * t, 8), :] = terms[0] + terms[1] + terms[2]


def split(value):
    high = value.astype(jnp.bfloat16)
    return high, (value - high.astype(jnp.float32)).astype(jnp.bfloat16)


def local_kernel(nx, ny, nz, block, half, rows, slots, scale, position, owner, m_ref, cw, xb, xa, yb, ya, zb, za,
                 out, mt, gt, hbuf, sbuf, rhs, ext, eyt, ezt):
    width = m_ref.shape[-1]
    pairs = width * (width + 1) // 2
    cells = nx * ny * nz
    gradient_tables(nx, ny, nz, m_ref, xb, xa, yb, ya, zb, za, mt, gt, ext, eyt, ezt)
    weight = cw[...] * scale
    for a in range(3):
        high, low = split(m_ref[a, :, pl.ds(0, TEST)] * weight)
        rhs[pl.ds(a * cells, cells), :] = jnp.concatenate([high, low], axis=1)
        rhs[pl.ds((3 + a) * cells, cells), :] = jnp.concatenate([high, jnp.zeros_like(low)], axis=1)
    pair_products(width, mt, gt, hbuf)

    @pl.loop(0, pairs // CHUNK)
    def _(c):
        here = pl.ds(pl.multiple_of(c * CHUNK, 16), CHUNK)
        parts = [split(hbuf[a, here, :]) for a in range(3)]
        left = jnp.concatenate([h for h, _ in parts] + [l for _, l in parts], axis=1)
        both = jnp.dot(left, rhs[...], preferred_element_type=jnp.float32)
        sbuf[here, :] = both + pltpu.roll(both, TEST, 1)

    spare = sbuf.shape[0] - pairs
    sbuf[pl.ds(pairs, spare), :] = jnp.zeros((spare, LANES), jnp.float32)
    first = lax.broadcasted_iota(jnp.int32, (rows, LANES), 1) < TEST

    @pl.loop(0, slots)
    def _(s):
        start = owner[s] * block
        low = sbuf[pl.ds(start, rows), :]
        high = sbuf[pl.ds(start + half, rows), :]
        out[position(s)] = jnp.where(first, low, high)


def local_tensor(modes, cell_weight, pair_owner, total_cells, block, position):
    _, nx, ny, nz, width = modes.shape
    cells = nx * ny * nz
    slots = pair_owner.shape[0]
    half = (block + 1) // 2
    rows = (half + 7) // 8 * 8
    xb, xa = halo(modes, "gx", 1, True)
    yb, ya = halo(modes, "gy", 2, True)
    zb, za = halo(modes, "gz", 3, False)
    flat = lambda v: v.reshape(3, -1, width)
    scale = 1.0 / math.sqrt(3.0 * total_cells)
    pairs = width * (width + 1) // 2
    sbuf_rows = (slots * block + half + rows + 7) // 8 * 8
    vmem = pl.BlockSpec(memory_space=pltpu.VMEM)
    return pl.pallas_call(
        functools.partial(local_kernel, nx, ny, nz, block, half, rows, slots, scale, position),
        out_shape=jax.ShapeDtypeStruct((slots, rows, LANES), jnp.float32),
        in_specs=[pl.BlockSpec(memory_space=pltpu.SMEM)] + [vmem] * 8,
        out_specs=vmem,
        scratch_shapes=[
            pltpu.VMEM((3, width + 8, cells), jnp.float32),
            pltpu.VMEM((9, width + 8, cells), jnp.float32),
            pltpu.VMEM((3, pairs + 8, cells), jnp.float32),
            pltpu.VMEM((sbuf_rows, LANES), jnp.float32),
            pltpu.VMEM((6 * cells, LANES), jnp.bfloat16),
            pltpu.VMEM((cells + 2 * ny * nz, width), jnp.float32),
            pltpu.VMEM((nx, ny * nz + 2 * nz, width), jnp.float32),
            pltpu.VMEM((2, cells + 16, width), jnp.float32),
        ],
        compiler_params=pltpu.CompilerParams(vmem_limit_bytes=48 * 1024 * 1024),
    )(pair_owner, flat(modes), cell_weight.reshape(cells, 1), flat(xb), flat(xa), flat(yb), flat(ya), flat(zb), flat(za))


def shards(modes, cell_weight, pair_owner):
    width = modes.shape[4]
    owners = lax.axis_size("gx") * lax.axis_size("gy") * lax.axis_size("gz")
    total_cells = modes.shape[1] * modes.shape[2] * modes.shape[3] * owners
    block = (width * (width + 1) // 2 + owners - 1) // owners
    half = (block + 1) // 2
    folded = local_tensor(modes, cell_weight, pair_owner, total_cells, block, lambda s: s)
    mine = lax.psum_scatter(folded, ("gx", "gy", "gz"), scatter_dimension=0, tiled=True)
    mine = lax.optimization_barrier(mine)[0, :half].reshape(half, 2, TEST).transpose(2, 1, 0)
    return mine.reshape(TEST, 2 * half)[:, :block]


def solution(mesh):
    placed = (P("groups", "gx", "gy", "gz", None), P("gx", "gy", "gz"), P())
    return jax.shard_map(
        shards,
        mesh=mesh,
        in_specs=placed,
        out_specs=P("groups", ("gx", "gy", "gz")),
        check_vma=False,
    )
```

time: 342 us -> 188 us (0.55)
  local copies, waits for them, and re-layouts: 152 us -> 7.09 us
  waiting for transfers between devices: 5.65 us -> 141 us
  blocking collectives: 82.5 us -> 0 us
  matrix products: 45.8 us -> 0 us
  other arithmetic: 42.8 us -> 0 us
  Pallas kernels: 0 us -> 14.7 us
  between operations: 0.33 us -> 13.5 us
    unnamed x2, waiting for transfers between devices: 2.07 us -> 137 us
    gather x6 -> x0, local copies, waits for them, and re-layouts: 129 us -> none  [the longest x1 42.8 us: shards(): index_j = jnp.take(table_j, clipped)]
    unnamed x1 -> x0, blocking collectives: 82.5 us -> none
    dot_general x16 -> x0, matrix products: 45.8 us -> none  [the longest x8 28.2 us: one_block(): jnp.einsum('ibxk,bxj->ijk', zeta, mode_flat, precision=lax.Precision.HIGH...]
    lt x1 -> x0, other arithmetic: 15.8 us -> none  [shards(): valid = pair_index < pair_total]
    pallas_call x0 -> x1, Pallas kernels: none -> 14.7 us  [local_tensor(): pl.pallas_call(functools.partial(local_kernel, nx, ny, nz, block, half, r...]
    mul x6 -> x0, local copies, waits for them, and re-layouts: 12.8 us -> none  [the longest x2 12.2 us: shards(): tensor = assemble(mode_flat, grad_flat, weight_flat, TEST, 8) * scale]
    select_n x3 -> x0, other arithmetic: 12.3 us -> none  [the longest x1 12 us: shards(): partial_terms = jnp.where(valid[None, :], summed, jnp.float32(0.0))]
  transfers between devices with their start and end apart: 8 -> 7, of which waited for: 5 -> 2; matrix products, arithmetic and copies ran while one was open for 34% -> 2% of each run, Pallas kernels for 0% -> 0%
where the time goes in v1:
time: 188 us
  waiting for transfers between devices  141 us (75%)
  Pallas kernels  14.7 us (8%)
  between operations  13.5 us (7%)
  starting transfers between devices  11.9 us (6%)
  local copies, waits for them, and re-layouts  7.09 us (4%)
    unnamed x2, waiting for transfers between devices  137 us
    pallas_call x1, Pallas kernels, local_tensor(): pl.pallas_call(functools.partial(local_kernel, nx, ny, nz, block, half, r...  14.7 us
    ppermute x6, starting transfers between devices, halo(): return (lax.ppermute(last, axis, up), lax.ppermute(leading, axis, down))  11.9 us
    ppermute x6, waiting for transfers between devices, halo(): return (lax.ppermute(last, axis, up), lax.ppermute(leading, axis, down))  3.86 us
  transfers between devices with their start and end apart: 7, of which 2 were waited for; matrix products, arithmetic and copies ran while one was open for 2% of the time, Pallas kernels for 0%

profile of v1, /device:TPU:0, one launch (start us, length us, event | category | flops | bytes accessed | tf_op | source)
XLA Modules:
  0.0 187.7 jit_solution(15281730691605585325)
XLA Ops:
  6.5 0.0 reduce-scatter.5.cloned.1.call-start
  6.5 0.8 fusion.1
  7.3 3.9 %collective-permute-start.3 = (f32[3,4,1,4,128]{4,3,2,1,0:T(4,128)S(1)}, f32[3,4,1,4,128]{4,3,2,1,0:T(4,128)S(1)}, u32[]{:S(2)}, u32[]{:S(2)}) collective-permute-start(f32[3,4,1,4,128]{4,3,2,1,0:T(4,128)S(1)} %get-tuple-element.7), channel_id=1, source_target_pairs={{2,0},{4,2},{6,4},{0,6},{3,1},{5,3},{7,5},{1,7},{10,8},{12,10},{14... | collective-permute-start | bytes 73736 | tf_op jit(solution)/shard_map/ppermute | solution.py:21
  11.2 0.8 fusion.2
  12.0 3.6 %collective-permute-start.1 = (f32[3,1,8,4,128]{4,3,2,1,0:T(4,128)S(1)}, f32[3,1,8,4,128]{4,3,2,1,0:T(4,128)S(1)}, u32[]{:S(2)}, u32[]{:S(2)}) collective-permute-start(f32[3,1,8,4,128]{4,3,2,1,0:T(4,128)S(1)} %get-tuple-element.9), channel_id=1, source_target_pairs={{8,0},{16,8},{24,16},{0,24},{9,1},{17,9},{25,17},{1,25},{10,2},{18... | collective-permute-start | bytes 147464 | tf_op jit(solution)/shard_map/ppermute | solution.py:21
  15.7 0.0 collective-permute-start
  15.7 1.1 fusion
  16.8 1.3 collective-permute-start.5
  18.1 3.0 %collective-permute-start.4 = (f32[3,4,8,1,128]{4,3,2,1,0:T(1,128)S(1)}, f32[3,4,8,1,128]{4,3,2,1,0:T(1,128)S(1)}, u32[]{:S(2)}, u32[]{:S(2)}) collective-permute-start(f32[3,4,8,1,128]{4,3,2,1,0:T(1,128)S(1)} %get-tuple-element.6), channel_id=1, source_target_pairs={{0,1},{2,3},{4,5},{6,7},{8,9},{10,11},{12,13},{14,15},{16,17},{18,... | collective-permute-start | bytes 147464 | tf_op jit(solution)/shard_map/ppermute | solution.py:21
  21.1 0.0 collective-permute-done.3
  21.1 0.1 collective-permute-start.2
  21.2 0.8 copy.12
  22.0 0.1 reshape.36.cw
  22.1 3.8 %collective-permute-done.2 = f32[3,4,1,4,128]{4,3,2,1,0:T(4,128)S(1)} collective-permute-done((f32[3,4,1,4,128]{4,3,2,1,0:T(4,128)S(1)}, f32[3,4,1,4,128]{4,3,2,1,0:T(4,128)S(1)}, u32[]{:S(2)}, u32[]{:S(2)}) %collective-permute-start.2) | collective-permute-done | bytes 24608 | tf_op jit(solution)/shard_map/ppermute | solution.py:21
  25.9 0.0 collective-permute-done.1
  25.9 0.0 collective-permute-done
  25.9 0.0 collective-permute-done.5
  25.9 0.0 collective-permute-done.4
  25.9 0.0 copy-start
  25.9 0.9 copy-done
  26.9 0.0 copy-start.1
  26.9 0.7 copy-done.1
  27.5 14.7 %shard_map.37 = f32[32,136,128]{2,1,0:T(8,128)} custom-call(s32[32]{0:T(128)S(1)} %copy-done.1, f32[3,128,128]{2,1,0:T(8,128)S(1)} %bitcast.9, f32[128,1]{1,0:T(8,128)S(1)} %reshape.36.cw, f32[3,32,128]{2,1,0:T(8,128)S(1)} %bitcast.11, f32[3,32,128]{2,1,0:T(8,128)S(1)} %bitcast.10, f32[3,16,128]{2,1,0:T(8,128)S(1)} %bitcast.15, f32[3,16,128]{2,1,0:T(8,128)S(1)} %bitcast.14, ...), custom_call_target="tpu_custom_call" | custom-call | tf_op jit(solution)/shard_map/pallas_call | solution.py:125
  42.2 0.0 reduce-scatter.5.cloned.1.call-update
  42.2 136.7 %reduce-scatter.5.cloned.1.call-done = f32[1,136,128]{2,1,0:T(8,128)} async-done(((f32[32,136,128]{2,1,0:T(8,128)}), f32[1,136,128]{2,1,0:T(8,128)}) %reduce-scatter.5.cloned.1.call-update) | async-done | bytes 69648
  178.9 1.0 reshape_squeeze.3
  180.0 0.1 copy.14
  180.1 0.8 reshape.35
Async XLA Ops:
  6.5 172.4 %reduce-scatter.5.cloned.1.call-start = ((), (), s32[]{:S(2)}) async-start(), calls=%async_computation.1 | async-start | bytes 2297856
  7.3 13.8 %collective-permute-start.3 = (f32[3,4,1,4,128]{4,3,2,1,0:T(4,128)S(1)}, f32[3,4,1,4,128]{4,3,2,1,0:T(4,128)S(1)}, u32[]{:S(2)}, u32[]{:S(2)}) collective-permute-start(f32[3,4,1,4,128]{4,3,2,1,0:T(4,128)S(1)} %get-tuple-element.7), channel_id=1, source_target_pairs={{2,0},{4,2},{6,4},{0,6},{3,1},{5,3},{7,5},{1,7},{10,8},{12,10},{14... | collective-permute-start | bytes 73736 | tf_op jit(solution)/shard_map/ppermute | solution.py:21
  12.0 13.9 %collective-permute-start.1 = (f32[3,1,8,4,128]{4,3,2,1,0:T(4,128)S(1)}, f32[3,1,8,4,128]{4,3,2,1,0:T(4,128)S(1)}, u32[]{:S(2)}, u32[]{:S(2)}) collective-permute-start(f32[3,1,8,4,128]{4,3,2,1,0:T(4,128)S(1)} %get-tuple-element.9), channel_id=1, source_target_pairs={{8,0},{16,8},{24,16},{0,24},{9,1},{17,9},{25,17},{1,25},{10,2},{18... | collective-permute-start | bytes 147464 | tf_op jit(solution)/shard_map/ppermute | solution.py:21
  15.7 10.3 %collective-permute-start = (f32[3,1,8,4,128]{4,3,2,1,0:T(4,128)S(1)}, f32[3,1,8,4,128]{4,3,2,1,0:T(4,128)S(1)}, u32[]{:S(2)}, u32[]{:S(2)}) collective-permute-start(f32[3,1,8,4,128]{4,3,2,1,0:T(4,128)S(1)} %get-tuple-element.10), channel_id=1, source_target_pairs={{0,8},{8,16},{16,24},{24,0},{1,9},{9,17},{17,25},{25,1},{2,10},{10... | collective-permute-start | bytes 147464 | tf_op jit(solution)/shard_map/ppermute | solution.py:21
  16.8 9.1 %collective-permute-start.5 = (f32[3,4,8,1,128]{4,3,2,1,0:T(1,128)S(1)}, f32[3,4,8,1,128]{4,3,2,1,0:T(1,128)S(1)}, u32[]{:S(2)}, u32[]{:S(2)}) collective-permute-start(f32[3,4,8,1,128]{4,3,2,1,0:T(1,128)S(1)} %get-tuple-element.5), channel_id=1, source_target_pairs={{1,0},{3,2},{5,4},{7,6},{9,8},{11,10},{13,12},{15,14},{17,16},{19,... | collective-permute-start | bytes 147464 | tf_op jit(solution)/shard_map/ppermute | solution.py:21
  18.1 7.8 %collective-permute-start.4 = (f32[3,4,8,1,128]{4,3,2,1,0:T(1,128)S(1)}, f32[3,4,8,1,128]{4,3,2,1,0:T(1,128)S(1)}, u32[]{:S(2)}, u32[]{:S(2)}) collective-permute-start(f32[3,4,8,1,128]{4,3,2,1,0:T(1,128)S(1)} %get-tuple-element.6), channel_id=1, source_target_pairs={{0,1},{2,3},{4,5},{6,7},{8,9},{10,11},{12,13},{14,15},{16,17},{18,... | collective-permute-start | bytes 147464 | tf_op jit(solution)/shard_map/ppermute | solution.py:21
  21.1 4.8 %collective-permute-start.2 = (f32[3,4,1,4,128]{4,3,2,1,0:T(4,128)S(1)}, f32[3,4,1,4,128]{4,3,2,1,0:T(4,128)S(1)}, u32[]{:S(2)}, u32[]{:S(2)}) collective-permute-start(f32[3,4,1,4,128]{4,3,2,1,0:T(4,128)S(1)} %get-tuple-element.8), channel_id=1, source_target_pairs={{0,2},{2,4},{4,6},{6,0},{1,3},{3,5},{5,7},{7,1},{8,10},{10,12},{12... | collective-permute-start | bytes 73736 | tf_op jit(solution)/shard_map/ppermute | solution.py:21
  25.9 0.9 copy-start
  26.9 0.7 copy-start.1
Sparse Core Ops, SparseCore 0:
  42.4 136.5 reduce-scatter.4

commit v2 on v1

--- a/solution.py
+++ b/solution.py
@@ -141,16 +141,131 @@
     )(pair_owner, flat(modes), cell_weight.reshape(cells, 1), flat(xb), flat(xa), flat(yb), flat(ya), flat(zb), flat(za))
 
 
+def bit_of(value, bit):
+    return lax.rem(value // (1 << bit), 2)
+
+
+def owned_kernel(nx, ny, nz, block, part, out, acc, from_core, from_gy, from_gx, core_send, core_recv, gy_send, gy_recv,
+                 gx_send, gx_recv):
+    cx, cy, cz = (lax.axis_index(name) for name in ("gx", "gy", "gz"))
+    bits = ny.bit_length() - 1
+    other = 1 - cz
+    mine = [bit_of(cy, b) for b in range(bits)]
+
+    def position(mask):
+        return sum((1 - mine[b] if mask >> b & 1 else mine[b]) * (1 << b) for b in range(bits))
+
+    barrier = pltpu.get_barrier_semaphore()
+    partners = [{"gz": other}] + [{"gy": position(1 << b)} for b in range(bits)]
+    partners += [{"gx": lax.rem(cx + d, nx)} for d in range(1, nx)]
+    for partner in partners:
+        pl.semaphore_signal(barrier, inc=1, device_id=partner, device_id_type=pl.DeviceIdType.MESH)
+    pl.semaphore_wait(barrier, len(partners))
+
+    def remote(src, dst, send, recv, device):
+        return pltpu.make_async_remote_copy(
+            src_ref=src, dst_ref=dst, send_sem=send, recv_sem=recv, device_id=device,
+            device_id_type=pl.DeviceIdType.MESH,
+        )
+
+    orders = [list(range(bits)), list(reversed(range(bits)))]
+
+    def rank(h, mask):
+        return sum((mask >> b & 1) << (bits - 1 - k) for k, b in enumerate(orders[h]))
+
+    sequence = [sorted(range(ny), key=lambda m: -rank(h, m)) for h in range(2)]
+    pending = []
+    first = {}
+    for at in range(ny):
+        for h in range(2):
+            m = sequence[h][at]
+            copy = remote(part.at[h, other, position(m)], from_core.at[h, m], core_send.at[h, m], core_recv.at[h, m],
+                          {"gz": other})
+            copy.start()
+            first[h, m] = copy
+            pending.append(copy)
+
+    def step_of(h, mask):
+        return next(k for k, b in enumerate(orders[h]) if mask >> b & 1)
+
+    hops = {}
+
+    def send(h, m):
+        b = orders[h][step_of(h, m)]
+        copy = remote(acc.at[h, m], from_gy.at[h, m], gy_send.at[h, m], gy_recv.at[h, m], {"gy": position(1 << b)})
+        copy.start()
+        hops[h, m] = copy
+        pending.append(copy)
+
+    for at in range(ny):
+        for h in range(2):
+            m = sequence[h][at]
+            first[h, m].wait_recv()
+            acc[h, m] = part[h, cz, position(m)] + from_core[h, m]
+            if m and step_of(h, m) == 0:
+                send(h, m)
+    for k in range(bits):
+        for at in range(ny):
+            for h in range(2):
+                m = sequence[h][at]
+                if m and step_of(h, m) == k:
+                    hops[h, m].wait_recv()
+                    left = m ^ (1 << orders[h][k])
+                    acc[h, left] = acc[h, left] + from_gy[h, m]
+                    if left and step_of(h, left) == k + 1:
+                        send(h, left)
+    lines = []
+    for d in range(1, nx):
+        to = lax.rem(cx + d, nx)
+        copy = remote(acc.at[to // (nx // 2), 0, lax.rem(to, nx // 2)], from_gx.at[d - 1], gx_send.at[d - 1],
+                      gx_recv.at[d - 1], {"gx": to})
+        copy.start()
+        lines.append(copy)
+        pending.append(copy)
+    total = acc[cx // (nx // 2), 0, lax.rem(cx, nx // 2)]
+    for d in range(1, nx):
+        lines[d - 1].wait_recv()
+        total = total + from_gx[d - 1]
+    half = (block + 1) // 2
+    turned = total.T
+    out[...] = jnp.concatenate([turned[:TEST, :half], turned[TEST:, :block - half]], axis=1)
+    for copy in pending:
+        copy.wait_send()
+
+
+def owned_block(part, block):
+    _, nz, ny, hx, rows, _ = part.shape
+    nx = 2 * hx
+    piece = (2, ny, hx, rows, LANES)
+    vmem = pl.BlockSpec(memory_space=pltpu.VMEM)
+    dma = pltpu.SemaphoreType.DMA
+    return pl.pallas_call(
+        functools.partial(owned_kernel, nx, ny, nz, block),
+        out_shape=jax.ShapeDtypeStruct((TEST, block), jnp.float32),
+        in_specs=[vmem],
+        out_specs=vmem,
+        scratch_shapes=[pltpu.VMEM(piece, jnp.float32)] * 3 + [pltpu.VMEM((nx - 1, rows, LANES), jnp.float32)]
+        + [dma((2, ny))] * 4 + [dma((nx - 1,))] * 2,
+        compiler_params=pltpu.CompilerParams(
+            collective_id=0, has_side_effects=True, vmem_limit_bytes=48 * 1024 * 1024
+        ),
+    )(part)
+
+
 def shards(modes, cell_weight, pair_owner):
     width = modes.shape[4]
-    owners = lax.axis_size("gx") * lax.axis_size("gy") * lax.axis_size("gz")
+    nx, ny, nz = (lax.axis_size(name) for name in ("gx", "gy", "gz"))
+    owners = nx * ny * nz
     total_cells = modes.shape[1] * modes.shape[2] * modes.shape[3] * owners
     block = (width * (width + 1) // 2 + owners - 1) // owners
-    half = (block + 1) // 2
-    folded = local_tensor(modes, cell_weight, pair_owner, total_cells, block, lambda s: s)
-    mine = lax.psum_scatter(folded, ("gx", "gy", "gz"), scatter_dimension=0, tiled=True)
-    mine = lax.optimization_barrier(mine)[0, :half].reshape(half, 2, TEST).transpose(2, 1, 0)
-    return mine.reshape(TEST, 2 * half)[:, :block]
+    hx = nx // 2
+
+    def position(s):
+        cx, cy, cz = s // (ny * nz), lax.rem(s // nz, ny), lax.rem(s, nz)
+        return (((cx // hx) * nz + cz) * ny + cy) * hx + lax.rem(cx, hx)
+
+    folded = local_tensor(modes, cell_weight, pair_owner, total_cells, block, position)
+    return owned_block(folded.reshape(2, nz, ny, hx, *folded.shape[1:]), block)
 
 
 def solution(mesh):

time: 188 us -> 56.8 us (0.30)
  waiting for transfers between devices: 141 us -> 3.86 us
  Pallas kernels: 14.7 us -> 34.8 us
  between operations: 13.5 us -> 0.08 us
    unnamed x2 -> x0, waiting for transfers between devices: 137 us -> none
    pallas_call x0 -> x1, Pallas kernels: none -> 21.2 us  [owned_block(): pl.pallas_call(functools.partial(owned_kernel, nx, ny, nz, block), out_sh...]
  transfers between devices with their start and end apart: 7 -> 6, of which waited for: 2 -> 1; matrix products, arithmetic and copies ran while one was open for 2% -> 5% of each run, Pallas kernels for 0% -> 0%
where the time goes in v2:
time: 56.8 us; the launch traced here: 56.5 us
  Pallas kernels  34.8 us (61%)
  starting transfers between devices  11.9 us (21%)
  local copies, waits for them, and re-layouts  5.8 us (10%)
  waiting for transfers between devices  3.86 us (7%)
    pallas_call x1, Pallas kernels, owned_block(): pl.pallas_call(functools.partial(owned_kernel, nx, ny, nz, block), out_sh...  21.2 us
    pallas_call x1, Pallas kernels, local_tensor(): pl.pallas_call(functools.partial(local_kernel, nx, ny, nz, block, half, r...  13.6 us
    ppermute x6, starting transfers between devices, halo(): return (lax.ppermute(last, axis, up), lax.ppermute(leading, axis, down))  11.9 us
    ppermute x6, waiting for transfers between devices, halo(): return (lax.ppermute(last, axis, up), lax.ppermute(leading, axis, down))  3.86 us
    unnamed x6, local copies, waits for them, and re-layouts  3.01 us
    slice x3, local copies, waits for them, and re-layouts, halo(): leading = lax.slice_in_dim(value, 0, 1, axis=dim)  2.71 us
  transfers between devices with their start and end apart: 6, of which 1 were waited for; matrix products, arithmetic and copies ran while one was open for 5% of the time, Pallas kernels for 0%

profile of v2, /device:TPU:0, one launch (start us, length us, event | category | flops | bytes accessed | tf_op | source)
XLA Modules:
  0.0 56.5 jit_solution(16146171783736078170)
XLA Ops:
  0.0 0.8 %fusion.1 = (f32[3,4,1,4,128]{4,3,2,1,0:T(4,128)S(1)}, f32[3,4,1,4,128]{4,3,2,1,0:T(4,128)S(1)}) fusion(f32[3,4,8,4,128]{4,3,2,1,0:T(4,128)} %param.3), kind=kLoop, calls=%fused_computation.1 | loop fusion | bytes 98304 | tf_op jit(solution)/shard_map/slice | solution.py:20
  0.8 3.9 %collective-permute-start.3 = (f32[3,4,1,4,128]{4,3,2,1,0:T(4,128)S(1)}, f32[3,4,1,4,128]{4,3,2,1,0:T(4,128)S(1)}, u32[]{:S(2)}, u32[]{:S(2)}) collective-permute-start(f32[3,4,1,4,128]{4,3,2,1,0:T(4,128)S(1)} %get-tuple-element.7), channel_id=1, source_target_pairs={{2,0},{4,2},{6,4},{0,6},{3,1},{5,3},{7,5},{1,7},{10,8},{12,10},{14... | collective-permute-start | bytes 73736 | tf_op jit(solution)/shard_map/ppermute | solution.py:21
  4.7 0.8 %fusion.2 = (f32[3,1,8,4,128]{4,3,2,1,0:T(4,128)S(1)}, f32[3,1,8,4,128]{4,3,2,1,0:T(4,128)S(1)}) fusion(f32[3,4,8,4,128]{4,3,2,1,0:T(4,128)} %param.3), kind=kLoop, calls=%fused_computation.2 | loop fusion | bytes 196608 | tf_op jit(solution)/shard_map/slice | solution.py:20
  5.5 3.6 %collective-permute-start.1 = (f32[3,1,8,4,128]{4,3,2,1,0:T(4,128)S(1)}, f32[3,1,8,4,128]{4,3,2,1,0:T(4,128)S(1)}, u32[]{:S(2)}, u32[]{:S(2)}) collective-permute-start(f32[3,1,8,4,128]{4,3,2,1,0:T(4,128)S(1)} %get-tuple-element.9), channel_id=1, source_target_pairs={{8,0},{16,8},{24,16},{0,24},{9,1},{17,9},{25,17},{1,25},{10,2},{18... | collective-permute-start | bytes 147464 | tf_op jit(solution)/shard_map/ppermute | solution.py:21
  9.1 0.0 collective-permute-start
  9.1 1.1 %fusion = (f32[3,4,8,1,128]{4,3,2,1,0:T(1,128)S(1)}, f32[3,4,8,1,128]{4,3,2,1,0:T(1,128)S(1)}) fusion(f32[3,4,8,4,128]{4,3,2,1,0:T(4,128)} %param.3), kind=kLoop, calls=%fused_computation | loop fusion | bytes 196608 | tf_op jit(solution)/shard_map/slice | solution.py:20
  10.2 1.3 %collective-permute-start.5 = (f32[3,4,8,1,128]{4,3,2,1,0:T(1,128)S(1)}, f32[3,4,8,1,128]{4,3,2,1,0:T(1,128)S(1)}, u32[]{:S(2)}, u32[]{:S(2)}) collective-permute-start(f32[3,4,8,1,128]{4,3,2,1,0:T(1,128)S(1)} %get-tuple-element.5), channel_id=1, source_target_pairs={{1,0},{3,2},{5,4},{7,6},{9,8},{11,10},{13,12},{15,14},{17,16},{19,... | collective-permute-start | bytes 147464 | tf_op jit(solution)/shard_map/ppermute | solution.py:21
  11.5 3.0 %collective-permute-start.4 = (f32[3,4,8,1,128]{4,3,2,1,0:T(1,128)S(1)}, f32[3,4,8,1,128]{4,3,2,1,0:T(1,128)S(1)}, u32[]{:S(2)}, u32[]{:S(2)}) collective-permute-start(f32[3,4,8,1,128]{4,3,2,1,0:T(1,128)S(1)} %get-tuple-element.6), channel_id=1, source_target_pairs={{0,1},{2,3},{4,5},{6,7},{8,9},{10,11},{12,13},{14,15},{16,17},{18,... | collective-permute-start | bytes 147464 | tf_op jit(solution)/shard_map/ppermute | solution.py:21
  14.6 0.0 collective-permute-done.3
  14.6 0.1 collective-permute-start.2
  14.7 0.8 %copy.6 = f32[4,8,4]{2,1,0:T(8,128)S(1)} copy(f32[4,8,4]{1,2,0:T(4,128)} %param.4) | data formatting | bytes 1024 | tf_op args[1]
  15.5 0.1 reshape.36.cw
  15.5 3.8 %collective-permute-done.2 = f32[3,4,1,4,128]{4,3,2,1,0:T(4,128)S(1)} collective-permute-done((f32[3,4,1,4,128]{4,3,2,1,0:T(4,128)S(1)}, f32[3,4,1,4,128]{4,3,2,1,0:T(4,128)S(1)}, u32[]{:S(2)}, u32[]{:S(2)}) %collective-permute-start.2) | collective-permute-done | bytes 24608 | tf_op jit(solution)/shard_map/ppermute | solution.py:21
  19.4 0.0 collective-permute-done.1
  19.4 0.0 collective-permute-done
  19.4 0.0 collective-permute-done.5
  19.4 0.0 collective-permute-done.4
  19.4 0.0 copy-start
  19.4 0.9 %copy-done = f32[3,4,8,4,128]{4,3,2,1,0:T(4,128)S(1)} copy-done((f32[3,4,8,4,128]{4,3,2,1,0:T(4,128)S(1)}, f32[3,4,8,4,128]{4,3,2,1,0:T(4,128)}, u32[]{:S(2)}) %copy-start) | copy-done | bytes 196632
  20.3 0.0 copy-start.1
  20.3 0.7 %copy-done.1 = s32[32]{0:T(128)S(1)} copy-done((s32[32]{0:T(128)S(1)}, s32[32]{0:T(128)}, u32[]{:S(2)}) %copy-start.1) | copy-done | bytes 152
  21.0 13.6 %shard_map.37 = f32[32,136,128]{2,1,0:T(8,128)S(1)} custom-call(s32[32]{0:T(128)S(1)} %copy-done.1, f32[3,128,128]{2,1,0:T(8,128)S(1)} %bitcast.9, f32[128,1]{1,0:T(8,128)S(1)} %reshape.36.cw, f32[3,32,128]{2,1,0:T(8,128)S(1)} %bitcast.11, f32[3,32,128]{2,1,0:T(8,128)S(1)} %bitcast.10, f32[3,16,128]{2,1,0:T(8,128)S(1)} %bitcast.15, ...), custom_call_target="tpu_custom_call" | custom-call | tf_op jit(solution)/shard_map/pallas_call | solution.py:125
  34.6 21.2 %shard_map.38 = f32[64,258]{1,0:T(8,128)S(1)} custom-call(f32[2,2,4,2,136,128]{5,4,3,2,1,0:T(8,128)S(1)} %bitcast.8), custom_call_target="tpu_custom_call" | custom-call | tf_op jit(solution)/shard_map/pallas_call | solution.py:242
  55.8 0.6 %copy.9 = f32[64,258]{1,0:T(8,128)} copy(f32[64,258]{1,0:T(8,128)S(1)} %shard_map.38) | data formatting | bytes 132096
Async XLA Ops:
  0.8 13.8 %collective-permute-start.3 = (f32[3,4,1,4,128]{4,3,2,1,0:T(4,128)S(1)}, f32[3,4,1,4,128]{4,3,2,1,0:T(4,128)S(1)}, u32[]{:S(2)}, u32[]{:S(2)}) collective-permute-start(f32[3,4,1,4,128]{4,3,2,1,0:T(4,128)S(1)} %get-tuple-element.7), channel_id=1, source_target_pairs={{2,0},{4,2},{6,4},{0,6},{3,1},{5,3},{7,5},{1,7},{10,8},{12,10},{14... | collective-permute-start | bytes 73736 | tf_op jit(solution)/shard_map/ppermute | solution.py:21
  5.5 13.9 %collective-permute-start.1 = (f32[3,1,8,4,128]{4,3,2,1,0:T(4,128)S(1)}, f32[3,1,8,4,128]{4,3,2,1,0:T(4,128)S(1)}, u32[]{:S(2)}, u32[]{:S(2)}) collective-permute-start(f32[3,1,8,4,128]{4,3,2,1,0:T(4,128)S(1)} %get-tuple-element.9), channel_id=1, source_target_pairs={{8,0},{16,8},{24,16},{0,24},{9,1},{17,9},{25,17},{1,25},{10,2},{18... | collective-permute-start | bytes 147464 | tf_op jit(solution)/shard_map/ppermute | solution.py:21
  9.1 10.3 %collective-permute-start = (f32[3,1,8,4,128]{4,3,2,1,0:T(4,128)S(1)}, f32[3,1,8,4,128]{4,3,2,1,0:T(4,128)S(1)}, u32[]{:S(2)}, u32[]{:S(2)}) collective-permute-start(f32[3,1,8,4,128]{4,3,2,1,0:T(4,128)S(1)} %get-tuple-element.10), channel_id=1, source_target_pairs={{0,8},{8,16},{16,24},{24,0},{1,9},{9,17},{17,25},{25,1},{2,10},{10... | collective-permute-start | bytes 147464 | tf_op jit(solution)/shard_map/ppermute | solution.py:21
  10.2 9.1 %collective-permute-start.5 = (f32[3,4,8,1,128]{4,3,2,1,0:T(1,128)S(1)}, f32[3,4,8,1,128]{4,3,2,1,0:T(1,128)S(1)}, u32[]{:S(2)}, u32[]{:S(2)}) collective-permute-start(f32[3,4,8,1,128]{4,3,2,1,0:T(1,128)S(1)} %get-tuple-element.5), channel_id=1, source_target_pairs={{1,0},{3,2},{5,4},{7,6},{9,8},{11,10},{13,12},{15,14},{17,16},{19,... | collective-permute-start | bytes 147464 | tf_op jit(solution)/shard_map/ppermute | solution.py:21
  11.5 7.8 %collective-permute-start.4 = (f32[3,4,8,1,128]{4,3,2,1,0:T(1,128)S(1)}, f32[3,4,8,1,128]{4,3,2,1,0:T(1,128)S(1)}, u32[]{:S(2)}, u32[]{:S(2)}) collective-permute-start(f32[3,4,8,1,128]{4,3,2,1,0:T(1,128)S(1)} %get-tuple-element.6), channel_id=1, source_target_pairs={{0,1},{2,3},{4,5},{6,7},{8,9},{10,11},{12,13},{14,15},{16,17},{18,... | collective-permute-start | bytes 147464 | tf_op jit(solution)/shard_map/ppermute | solution.py:21
  14.6 4.8 %collective-permute-start.2 = (f32[3,4,1,4,128]{4,3,2,1,0:T(4,128)S(1)}, f32[3,4,1,4,128]{4,3,2,1,0:T(4,128)S(1)}, u32[]{:S(2)}, u32[]{:S(2)}) collective-permute-start(f32[3,4,1,4,128]{4,3,2,1,0:T(4,128)S(1)} %get-tuple-element.8), channel_id=1, source_target_pairs={{0,2},{2,4},{4,6},{6,0},{1,3},{3,5},{5,7},{7,1},{8,10},{10,12},{12... | collective-permute-start | bytes 73736 | tf_op jit(solution)/shard_map/ppermute | solution.py:21
  19.4 0.9 %copy-start = (f32[3,4,8,4,128]{4,3,2,1,0:T(4,128)S(1)}, f32[3,4,8,4,128]{4,3,2,1,0:T(4,128)}, u32[]{:S(2)}) copy-start(f32[3,4,8,4,128]{4,3,2,1,0:T(4,128)} %param.3) | copy-start | bytes 589828
  20.3 0.7 %copy-start.1 = (s32[32]{0:T(128)S(1)}, s32[32]{0:T(128)}, u32[]{:S(2)}) copy-start(s32[32]{0:T(128)} %owner.1) | copy-start | bytes 388

commit v3 on v1

v3 whole, which is shorter than its diff:
```python
import functools
import math
import jax
import jax.numpy as jnp
from jax import lax
from jax.experimental import pallas as pl
from jax.experimental.pallas import tpu as pltpu
from jax.sharding import PartitionSpec as P

TEST = 64
LANES = 128
CHUNK = 688
STAGES = 4


def bounds(rows):
    tiles = rows // 8
    stages = min(STAGES, tiles)
    cuts = [8 * (tiles * c // stages) for c in range(stages + 1)]
    return [(a, b - a) for a, b in zip(cuts, cuts[1:])]


def transposed_gradients(lx, ly, lz, level, m_ref, faces, gt, ext, eyt, ezt):
    cells, plane, width = lx * ly * lz, ly * lz, m_ref.shape[-1]
    x_before, x_after, y_before, y_after, z_face = faces
    for a in range(3):
        m = m_ref[a].reshape(cells, width)
        ext[pl.ds(0, plane), :] = x_before[a, 0]
        ext[pl.ds(plane, cells), :] = m
        ext[pl.ds(plane + cells, plane), :] = x_after[a, 0]
        step = (ext[pl.ds(2 * plane, cells), :] - ext[pl.ds(0, cells), :]) * 0.5
        gt[3 * a, pl.ds(0, width), :] = step.T
        for x in range(lx):
            eyt[x, pl.ds(0, lz), :] = y_before[a, x, pl.ds(8 - lz, lz), :]
            eyt[x, pl.ds(lz, plane), :] = m_ref[a, x]
            eyt[x, pl.ds(lz + plane, lz), :] = y_after[a, x, pl.ds(0, lz), :]
        step = (eyt[:, pl.ds(2 * lz, plane), :] - eyt[:, pl.ds(0, plane), :]) * 0.5
        gt[3 * a + 1, pl.ds(0, width), :] = step.reshape(cells, width).T
        ezt[0, pl.ds(8, cells), :] = m
        ezt[1, pl.ds(0, cells), :] = ezt[0, pl.ds(9, cells), :]
        ezt[0, pl.ds(0, cells), :] = ezt[0, pl.ds(7, cells), :]
        ezt[0, pl.ds(0, lx * ly, stride=lz), :] = jnp.where(level == 1, z_face[a], 0.0)
        ezt[1, pl.ds(lz - 1, lx * ly, stride=lz), :] = jnp.where(level == 0, z_face[a], 0.0)
        step = (ezt[1, pl.ds(0, cells), :] - ezt[0, pl.ds(0, cells), :]) * 0.5
        gt[3 * a + 2, pl.ds(0, width), :] = step.T
        for b in range(3):
            gt[3 * a + b, pl.ds(width, 8), :] = jnp.zeros((8, cells), jnp.float32)


def pair_products(width, mt, gt, hbuf):
    for group in range(width // 8):
        tiles = width // 8 - group

        @pl.loop(group * 8, group * 8 + 8)
        def _(j):
            start = j * width - (j * (j - 1)) // 2
            mj = [mt[b, pl.ds(j, 1), :] for b in range(3)]
            gj = [gt[c, pl.ds(j, 1), :] for c in range(9)]
            for t in range(tiles):
                mk = [mt[b, pl.ds(j + 8 * t, 8), :] for b in range(3)]
                for a in range(3):
                    terms = [
                        mj[b] * gt[3 * a + b, pl.ds(j + 8 * t, 8), :] + gj[3 * a + b] * mk[b]
                        for b in range(3)
                    ]
                    hbuf[a, pl.ds(start + 8 * t, 8), :] = terms[0] + terms[1] + terms[2]


def split(value):
    high = value.astype(jnp.bfloat16)
    return high, (value - high.astype(jnp.float32)).astype(jnp.bfloat16)


def bit_of(value, bit):
    return lax.rem(value // (1 << bit), 2)


def convective_kernel(mesh_shape, local_shape, block, scale, owner, m_ref, cw, out,
                      x_before, x_after, y_before, y_after, z_face, z_out, mt, gt, hbuf, sbuf, rhs, ext, eyt, ezt,
                      part, acc, from_core, from_gy, from_gx, face_send, face_recv,
                      core_send, core_recv, gy_send, gy_recv, gx_send, gx_recv):
    nx, ny, nz = mesh_shape
    lx, ly, lz = local_shape
    cells, plane, width = lx * ly * lz, ly * lz, m_ref.shape[-1]
    pairs = width * (width + 1) // 2
    half = (block + 1) // 2
    hx = nx // 2
    parts = bounds(acc.shape[3])
    cx, cy, cz = (lax.axis_index(name) for name in ("gx", "gy", "gz"))
    other = 1 - cz
    bits = ny.bit_length() - 1
    mine = [bit_of(cy, b) for b in range(bits)]

    def position(mask):
        return sum((1 - mine[b] if mask >> b & 1 else mine[b]) * (1 << b) for b in range(bits))

    pending = []

    def remote(src, dst, send, recv, device):
        copy = pltpu.make_async_remote_copy(
            src_ref=src, dst_ref=dst, send_sem=send, recv_sem=recv, device_id=device,
            device_id_type=pl.DeviceIdType.MESH,
        )
        copy.start()
        pending.append(copy)
        return copy

    barrier = pltpu.get_barrier_semaphore()
    partners = [{"gz": other}] + [{"gy": lax.rem(cy + d, ny)} for d in range(1, ny)]
    partners += [{"gx": lax.rem(cx + d, nx)} for d in range(1, nx)]
    for partner in partners:
        pl.semaphore_signal(barrier, inc=1, device_id=partner, device_id_type=pl.DeviceIdType.MESH)
    for a in range(3):
        m = m_ref[a].reshape(cells, width)
        ezt[0, pl.ds(0, cells), :] = m
        top = ezt[0, pl.ds(lz - 1, lx * ly, stride=lz), :]
        bottom = ezt[0, pl.ds(0, lx * ly, stride=lz), :]
        z_out[a] = jnp.where(cz == 0, top, bottom)
    pl.semaphore_wait(barrier, len(partners))

    arrivals = [
        remote(m_ref.at[:, pl.ds(lx - 1, 1)], x_before, face_send.at[0], face_recv.at[0], {"gx": lax.rem(cx + 1, nx)}),
        remote(m_ref.at[:, pl.ds(0, 1)], x_after, face_send.at[1], face_recv.at[1], {"gx": lax.rem(cx + nx - 1, nx)}),
        remote(m_ref.at[:, :, pl.ds(plane - 8, 8)], y_before, face_send.at[2], face_recv.at[2],
               {"gy": lax.rem(cy + 1, ny)}),
        remote(m_ref.at[:, :, pl.ds(0, 8)], y_after, face_send.at[3], face_recv.at[3],
               {"gy": lax.rem(cy + ny - 1, ny)}),
        remote(z_out, z_face, face_send.at[4], face_recv.at[4], {"gz": other}),
    ]
    weight = cw[...] * scale
    for a in range(3):
        m = m_ref[a].reshape(cells, width)
        mt[a, pl.ds(0, width), :] = m.T
        mt[a, pl.ds(width, 8), :] = jnp.zeros((8, cells), jnp.float32)
        high, low = split(m[:, :TEST] * weight)
        rhs[pl.ds(a * cells, cells), :] = jnp.concatenate([high, low], axis=1)
        rhs[pl.ds((3 + a) * cells, cells), :] = jnp.concatenate([high, jnp.zeros_like(low)], axis=1)
    spare = sbuf.shape[0] - pairs
    sbuf[pl.ds(pairs, spare), :] = jnp.zeros((spare, LANES), jnp.float32)
    for copy in arrivals:
        copy.wait_recv()
    transposed_gradients(lx, ly, lz, cz, m_ref, (x_before, x_after, y_before, y_after, z_face), gt, ext, eyt, ezt)
    pair_products(width, mt, gt, hbuf)

    @pl.loop(0, pairs // CHUNK)
    def _(c):
        here = pl.ds(pl.multiple_of(c * CHUNK, 16), CHUNK)
        pieces = [split(hbuf[a, here, :]) for a in range(3)]
        left = jnp.concatenate([h for h, _ in pieces] + [l for _, l in pieces], axis=1)
        both = jnp.dot(left, rhs[...], preferred_element_type=jnp.float32)
        sbuf[here, :] = both + pltpu.roll(both, TEST, 1)

    def folded(h, mask, level, t, rows_from, count):
        slot = ((h * hx + t) * ny + position(mask)) * nz + level
        start = owner[slot] * block + rows_from
        first = lax.broadcasted_iota(jnp.int32, (count, LANES), 1) < TEST
        return jnp.where(first, sbuf[pl.ds(start, count), :], sbuf[pl.ds(start + half, count), :])

    orders = [list(range(bits)), list(reversed(range(bits)))]

    def rank(h, mask):
        return sum((mask >> b & 1) << (bits - 1 - k) for k, b in enumerate(orders[h]))

    def step_of(h, mask):
        return next(k for k, b in enumerate(orders[h]) if mask >> b & 1)

    sequence = [(h, m) for at in range(ny) for h, m in
                [(h, sorted(range(ny), key=lambda m: -rank(h, m))[at]) for h in range(2)]]
    first_hop, hops, lines = {}, {}, {}

    def send(c, h, m):
        b = orders[h][step_of(h, m)]
        rows = pl.ds(*parts[c])
        hops[c, h, m] = remote(acc.at[h, m, :, rows], from_gy.at[h, m, :, rows], gy_send.at[c, h, m],
                               gy_recv.at[c, h, m], {"gy": position(1 << b)})

    def across_cores(c):
        rows_from, count = parts[c]
        rows = pl.ds(rows_from, count)
        for h, m in sequence:
            @pl.loop(0, hx)
            def _(t):
                part[h, m, t, rows, :] = folded(h, m, other, t, rows_from, count)

            first_hop[c, h, m] = remote(part.at[h, m, :, rows], from_core.at[h, m, :, rows], core_send.at[c, h, m],
                                        core_recv.at[c, h, m], {"gz": other})

    def chip_sums(c):
        rows_from, count = parts[c]
        rows = pl.ds(rows_from, count)
        for h, m in sequence:
            first_hop[c, h, m].wait_recv()

            @pl.loop(0, hx)
            def _(t):
                acc[h, m, t, rows, :] = folded(h, m, cz, t, rows_from, count) + from_core[h, m, t, rows, :]

            if m and step_of(h, m) == 0:
                send(c, h, m)

    def across_gy(c, k):
        rows = pl.ds(*parts[c])
        for h, m in sequence:
            if m and step_of(h, m) == k:
                hops[c, h, m].wait_recv()
                left = m ^ (1 << orders[h][k])
                acc[h, left, :, rows, :] = acc[h, left, :, rows, :] + from_gy[h, m, :, rows, :]
                if left and step_of(h, left) == k + 1:
                    send(c, h, left)
        if k == bits - 1:
            for d in range(1, nx):
                to = lax.rem(cx + d, nx)
                lines[c, d] = remote(acc.at[to // hx, 0, lax.rem(to, hx), rows], from_gx.at[d - 1, rows],
                                     gx_send.at[c, d - 1], gx_recv.at[c, d - 1], {"gx": to})

    stages = [across_cores, chip_sums] + [functools.partial(across_gy, k=k) for k in range(bits)]
    for wave in range(len(parts) + len(stages) - 1):
        for k, stage in enumerate(stages):
            if 0 <= wave - k < len(parts):
                stage(wave - k)
    sums = []
    for c, (rows_from, count) in enumerate(parts):
        rows = pl.ds(rows_from, count)
        total = acc[cx // hx, 0, lax.rem(cx, hx), rows, :]
        for d in range(1, nx):
            lines[c, d].wait_recv()
            total = total + from_gx[d - 1, rows, :]
        sums.append(total)
    turned = jnp.concatenate(sums, axis=0).T
    out[...] = jnp.concatenate([turned[:TEST, :half], turned[TEST:, :block - half]], axis=1)
    for copy in pending:
        copy.wait_send()


def shards(modes, cell_weight, pair_owner):
    _, lx, ly, lz, width = modes.shape
    nx, ny, nz = (lax.axis_size(name) for name in ("gx", "gy", "gz"))
    slots = nx * ny * nz
    cells, plane = lx * ly * lz, ly * lz
    pairs = width * (width + 1) // 2
    block = (pairs + slots - 1) // slots
    half = (block + 1) // 2
    rows = (half + 7) // 8 * 8
    hx = nx // 2
    scale = 1.0 / math.sqrt(3.0 * cells * slots)
    sbuf_rows = (slots * block + half + rows + 7) // 8 * 8
    stages = len(bounds(rows))
    vmem = pl.BlockSpec(memory_space=pltpu.VMEM)
    dma = pltpu.SemaphoreType.DMA

    def buffer(*shape):
        return pltpu.VMEM(shape, jnp.float32)

    return pl.pallas_call(
        functools.partial(convective_kernel, (nx, ny, nz), (lx, ly, lz), block, scale),
        out_shape=jax.ShapeDtypeStruct((TEST, block), jnp.float32),
        in_specs=[pl.BlockSpec(memory_space=pltpu.SMEM), vmem, vmem],
        out_specs=vmem,
        scratch_shapes=[
            buffer(3, 1, plane, width), buffer(3, 1, plane, width),
            buffer(3, lx, 8, width), buffer(3, lx, 8, width),
            buffer(3, lx * ly, width), buffer(3, lx * ly, width),
            buffer(3, width + 8, cells), buffer(9, width + 8, cells),
            buffer(3, pairs + 8, cells), buffer(sbuf_rows, LANES),
            pltpu.VMEM((6 * cells, LANES), jnp.bfloat16),
            buffer(cells + 2 * plane, width), buffer(lx, plane + 2 * lz, width), buffer(2, cells + 16, width),
            buffer(2, ny, hx, rows, LANES), buffer(2, ny, hx, rows, LANES),
            buffer(2, ny, hx, rows, LANES), buffer(2, ny, hx, rows, LANES),
            buffer(nx - 1, rows, LANES),
            dma((5,)), dma((5,)),
        ] + [dma((stages, 2, ny))] * 4 + [dma((stages, nx - 1))] * 2,
        compiler_params=pltpu.CompilerParams(
            collective_id=0, has_side_effects=True, vmem_limit_bytes=48 * 1024 * 1024
        ),
    )(pair_owner, modes.reshape(3, lx, plane, width), cell_weight.reshape(cells, 1))


def solution(mesh):
    placed = (P("groups", "gx", "gy", "gz", None), P("gx", "gy", "gz"), P())
    return jax.shard_map(
        shards,
        mesh=mesh,
        in_specs=placed,
        out_specs=P("groups", ("gx", "gy", "gz")),
        check_vma=False,
    )
```

time: 188 us -> 45.1 us (0.24)
  waiting for transfers between devices: 141 us -> 0 us
  Pallas kernels: 14.7 us -> 41.9 us
  between operations: 13.5 us -> 0.01 us
  starting transfers between devices: 11.9 us -> 0 us
  local copies, waits for them, and re-layouts: 7.09 us -> 3.01 us
    unnamed x2 -> x0, waiting for transfers between devices: 137 us -> none
    pallas_call x1, Pallas kernels: 14.7 us -> 41.9 us  [shards(): pl.pallas_call(functools.partial(convective_kernel, (nx, ny, nz), (lx, ly...]
    ppermute x6 -> x0, starting transfers between devices: 11.9 us -> none  [halo(): return (lax.ppermute(last, axis, up), lax.ppermute(leading, axis, down))]
    ppermute x6 -> x0, waiting for transfers between devices: 3.86 us -> none  [halo(): return (lax.ppermute(last, axis, up), lax.ppermute(leading, axis, down))]
    slice x3 -> x0, local copies, waits for them, and re-layouts: 2.71 us -> none  [halo(): leading = lax.slice_in_dim(value, 0, 1, axis=dim)]
  transfers between devices with their start and end apart: 7 -> 0, of which waited for: 2 -> 0; matrix products, arithmetic and copies ran while one was open for 2% -> 0% of each run, Pallas kernels for 0% -> 0%
where the time goes in v3:
time: 45.1 us; the launch traced here: 44.9 us
  Pallas kernels  41.9 us (93%)
  local copies, waits for them, and re-layouts  3.01 us (7%)
    pallas_call x1, Pallas kernels, shards(): pl.pallas_call(functools.partial(convective_kernel, (nx, ny, nz), (lx, ly...  41.9 us
    unnamed x6, local copies, waits for them, and re-layouts  2.94 us

profile of v3, /device:TPU:0, one launch (start us, length us, event | category | flops | bytes accessed | tf_op | source)
XLA Modules:
  0.0 44.9 jit_solution(8751936200447048882)
XLA Ops:
  0.0 0.8 %copy.6 = f32[4,8,4]{2,1,0:T(8,128)S(1)} copy(f32[4,8,4]{1,2,0:T(4,128)} %param.4) | data formatting | bytes 1024 | tf_op args[1]
  0.8 0.0 copy-start.1
  0.8 0.1 reshape.8.cw
  0.9 0.6 %copy-done.1 = s32[32]{0:T(128)S(1)} copy-done((s32[32]{0:T(128)S(1)}, s32[32]{0:T(128)}, u32[]{:S(2)}) %copy-start.1) | copy-done | bytes 152
  1.4 0.0 copy-start
  1.4 0.9 %copy-done = f32[3,4,8,4,128]{4,3,2,1,0:T(4,128)S(1)} copy-done((f32[3,4,8,4,128]{4,3,2,1,0:T(4,128)S(1)}, f32[3,4,8,4,128]{4,3,2,1,0:T(4,128)}, u32[]{:S(2)}) %copy-start) | copy-done | bytes 196632
  2.4 41.9 %shard_map.37 = f32[64,258]{1,0:T(8,128)S(1)} custom-call(s32[32]{0:T(128)S(1)} %copy-done.1, f32[3,4,32,128]{3,2,1,0:T(8,128)S(1)} %bitcast.1, f32[128,1]{1,0:T(8,128)S(1)} %reshape.8.cw), custom_call_target="tpu_custom_call" | custom-call | tf_op jit(solution)/shard_map/pallas_call | solution.py:254
  44.3 0.6 %copy.9 = f32[64,258]{1,0:T(8,128)} copy(f32[64,258]{1,0:T(8,128)S(1)} %shard_map.37) | data formatting | bytes 132096
Async XLA Ops:
  0.8 0.7 %copy-start.1 = (s32[32]{0:T(128)S(1)}, s32[32]{0:T(128)}, u32[]{:S(2)}) copy-start(s32[32]{0:T(128)} %owner.1) | copy-start | bytes 388
  1.4 0.9 %copy-start = (f32[3,4,8,4,128]{4,3,2,1,0:T(4,128)S(1)}, f32[3,4,8,4,128]{4,3,2,1,0:T(4,128)}, u32[]{:S(2)}) copy-start(f32[3,4,8,4,128]{4,3,2,1,0:T(4,128)} %param.3) | copy-start | bytes 589828

commit v4 on v3

--- a/solution.py
+++ b/solution.py
@@ -9,7 +9,6 @@
 
 TEST = 64
 LANES = 128
-CHUNK = 688
 STAGES = 4
 
 
@@ -75,8 +74,8 @@
     return lax.rem(value // (1 << bit), 2)
 
 
-def convective_kernel(mesh_shape, local_shape, block, scale, owner, m_ref, cw, out,
-                      x_before, x_after, y_before, y_after, z_face, z_out, mt, gt, hbuf, sbuf, rhs, ext, eyt, ezt,
+def convective_kernel(mesh_shape, local_shape, block, scale, owner, m_hbm, cw_hbm, out, m_ref, cw, load,
+                      x_before, x_after, y_before, y_after, z_face, z_out, mt, gt, hbuf, lhs, rhs, wide, ext, eyt, ezt,
                       part, acc, from_core, from_gy, from_gx, face_send, face_recv,
                       core_send, core_recv, gy_send, gy_recv, gx_send, gx_recv):
     nx, ny, nz = mesh_shape
@@ -105,11 +104,16 @@
         pending.append(copy)
         return copy
 
+    loads = [pltpu.make_async_copy(m_hbm, m_ref, load.at[0]), pltpu.make_async_copy(cw_hbm, cw, load.at[1])]
+    for copy in loads:
+        copy.start()
     barrier = pltpu.get_barrier_semaphore()
     partners = [{"gz": other}] + [{"gy": lax.rem(cy + d, ny)} for d in range(1, ny)]
     partners += [{"gx": lax.rem(cx + d, nx)} for d in range(1, nx)]
     for partner in partners:
         pl.semaphore_signal(barrier, inc=1, device_id=partner, device_id_type=pl.DeviceIdType.MESH)
+    for copy in loads:
+        copy.wait()
     for a in range(3):
         m = m_ref[a].reshape(cells, width)
         ezt[0, pl.ds(0, cells), :] = m
@@ -127,7 +131,12 @@
                {"gy": lax.rem(cy + ny - 1, ny)}),
         remote(z_out, z_face, face_send.at[4], face_recv.at[4], {"gz": other}),
     ]
-    weight = cw[...] * scale
+    for x in range(lx):
+        turned = cw[x].T * scale
+        for z in range(lz):
+            column = jnp.broadcast_to(turned[:, z:z + 1], (ly, LANES))
+            wide[pl.ds(x * plane + z, ly, stride=lz), :] = column
+    weight = wide[:, :TEST]
     for a in range(3):
         m = m_ref[a].reshape(cells, width)
         mt[a, pl.ds(0, width), :] = m.T
@@ -135,78 +144,67 @@
         high, low = split(m[:, :TEST] * weight)
         rhs[pl.ds(a * cells, cells), :] = jnp.concatenate([high, low], axis=1)
         rhs[pl.ds((3 + a) * cells, cells), :] = jnp.concatenate([high, jnp.zeros_like(low)], axis=1)
-    spare = sbuf.shape[0] - pairs
-    sbuf[pl.ds(pairs, spare), :] = jnp.zeros((spare, LANES), jnp.float32)
+    spare = hbuf.shape[1] - pairs
+    for a in range(3):
+        hbuf[a, pl.ds(pairs, spare), :] = jnp.zeros((spare, cells), jnp.float32)
     for copy in arrivals:
         copy.wait_recv()
     transposed_gradients(lx, ly, lz, cz, m_ref, (x_before, x_after, y_before, y_after, z_face), gt, ext, eyt, ezt)
     pair_products(width, mt, gt, hbuf)
 
-    @pl.loop(0, pairs // CHUNK)
-    def _(c):
-        here = pl.ds(pl.multiple_of(c * CHUNK, 16), CHUNK)
-        pieces = [split(hbuf[a, here, :]) for a in range(3)]
-        left = jnp.concatenate([h for h, _ in pieces] + [l for _, l in pieces], axis=1)
-        both = jnp.dot(left, rhs[...], preferred_element_type=jnp.float32)
-        sbuf[here, :] = both + pltpu.roll(both, TEST, 1)
-
-    def folded(h, mask, level, t, rows_from, count):
-        slot = ((h * hx + t) * ny + position(mask)) * nz + level
-        start = owner[slot] * block + rows_from
-        first = lax.broadcasted_iota(jnp.int32, (count, LANES), 1) < TEST
-        return jnp.where(first, sbuf[pl.ds(start, count), :], sbuf[pl.ds(start + half, count), :])
-
     orders = [list(range(bits)), list(reversed(range(bits)))]
-
-    def rank(h, mask):
-        return sum((mask >> b & 1) << (bits - 1 - k) for k, b in enumerate(orders[h]))
-
-    def step_of(h, mask):
-        return next(k for k, b in enumerate(orders[h]) if mask >> b & 1)
-
-    sequence = [(h, m) for at in range(ny) for h, m in
-                [(h, sorted(range(ny), key=lambda m: -rank(h, m))[at]) for h in range(2)]]
-    first_hop, hops, lines = {}, {}, {}
-
-    def send(c, h, m):
-        b = orders[h][step_of(h, m)]
-        rows = pl.ds(*parts[c])
-        hops[c, h, m] = remote(acc.at[h, m, :, rows], from_gy.at[h, m, :, rows], gy_send.at[c, h, m],
-                               gy_recv.at[c, h, m], {"gy": position(1 << b)})
-
-    def across_cores(c):
+    masks = [[sum((r >> (bits - 1 - k) & 1) << b for k, b in enumerate(orders[h])) for r in range(ny)] for h in range(2)]
+
+    def products(c, h, level, into):
         rows_from, count = parts[c]
-        rows = pl.ds(rows_from, count)
-        for h, m in sequence:
+        for r in range(ny):
             @pl.loop(0, hx)
             def _(t):
-                part[h, m, t, rows, :] = folded(h, m, other, t, rows_from, count)
-
-            first_hop[c, h, m] = remote(part.at[h, m, :, rows], from_core.at[h, m, :, rows], core_send.at[c, h, m],
-                                        core_recv.at[c, h, m], {"gz": other})
+                slot = ((h * hx + t) * ny + position(masks[h][r])) * nz + level
+                start = owner[slot] * block + rows_from
+                at = pl.ds(pl.multiple_of((r * hx + t) * 2 * count, 16), 2 * count)
+                for a in range(3):
+                    both = [hbuf[a, pl.ds(start, count), :], hbuf[a, pl.ds(start + half, count), :]]
+                    high, low = split(jnp.concatenate(both, axis=0))
+                    lhs[at, pl.ds(a * cells, cells)] = high
+                    lhs[at, pl.ds((3 + a) * cells, cells)] = low
+
+        result = jnp.dot(lhs[pl.ds(0, ny * hx * 2 * count), :], rhs[...], preferred_element_type=jnp.float32)
+        result = (result + pltpu.roll(result, TEST, 1)).reshape(ny, hx, 2, count, LANES)
+        first = lax.broadcasted_iota(jnp.int32, (ny, hx, count, LANES), 3) < TEST
+        into[h, :, :, pl.ds(rows_from, count), :] = jnp.where(first, result[:, :, 0], result[:, :, 1])
+
+    first_hop, hops, lines = {}, {}, {}
+
+    def send(c, h, k):
+        n = ny >> (k + 1)
+        rows = pl.ds(*parts[c])
+        hops[c, h, k] = remote(acc.at[h, pl.ds(n, n), :, rows], from_gy.at[h, pl.ds(n, n), :, rows],
+                               gy_send.at[c, h, k], gy_recv.at[c, h, k], {"gy": position(1 << orders[h][k])})
+
+    def across_cores(c):
+        rows = pl.ds(*parts[c])
+        for h in range(2):
+            products(c, h, other, part)
+            first_hop[c, h] = remote(part.at[h, :, :, rows], from_core.at[h, :, :, rows], core_send.at[c, h],
+                                     core_recv.at[c, h], {"gz": other})
 
     def chip_sums(c):
-        rows_from, count = parts[c]
-        rows = pl.ds(rows_from, count)
-        for h, m in sequence:
-            first_hop[c, h, m].wait_recv()
-
-            @pl.loop(0, hx)
-            def _(t):
-                acc[h, m, t, rows, :] = folded(h, m, cz, t, rows_from, count) + from_core[h, m, t, rows, :]
-
-            if m and step_of(h, m) == 0:
-                send(c, h, m)
+        rows = pl.ds(*parts[c])
+        for h in range(2):
+            products(c, h, cz, acc)
+            first_hop[c, h].wait_recv()
+            acc[h, :, :, rows, :] = acc[h, :, :, rows, :] + from_core[h, :, :, rows, :]
+            send(c, h, 0)
 
     def across_gy(c, k):
-        rows = pl.ds(*parts[c])
-        for h, m in sequence:
-            if m and step_of(h, m) == k:
-                hops[c, h, m].wait_recv()
-                left = m ^ (1 << orders[h][k])
-                acc[h, left, :, rows, :] = acc[h, left, :, rows, :] + from_gy[h, m, :, rows, :]
-                if left and step_of(h, left) == k + 1:
-                    send(c, h, left)
+        n = ny >> (k + 1)
+        rows = pl.ds(*parts[c])
+        for h in range(2):
+            hops[c, h, k].wait_recv()
+            acc[h, pl.ds(0, n), :, rows, :] = acc[h, pl.ds(0, n), :, rows, :] + from_gy[h, pl.ds(n, n), :, rows, :]
+            if k < bits - 1:
+                send(c, h, k + 1)
         if k == bits - 1:
             for d in range(1, nx):
                 to = lax.rem(cx + d, nx)
@@ -243,9 +241,12 @@
     rows = (half + 7) // 8 * 8
     hx = nx // 2
     scale = 1.0 / math.sqrt(3.0 * cells * slots)
-    sbuf_rows = (slots * block + half + rows + 7) // 8 * 8
+    table_rows = (slots * block + half + rows + 7) // 8 * 8
     stages = len(bounds(rows))
+    longest = max(count for _, count in bounds(rows))
+    bits = ny.bit_length() - 1
     vmem = pl.BlockSpec(memory_space=pltpu.VMEM)
+    hbm = pl.BlockSpec(memory_space=pltpu.HBM)
     dma = pltpu.SemaphoreType.DMA
 
     def buffer(*shape):
@@ -254,25 +255,26 @@
     return pl.pallas_call(
         functools.partial(convective_kernel, (nx, ny, nz), (lx, ly, lz), block, scale),
         out_shape=jax.ShapeDtypeStruct((TEST, block), jnp.float32),
-        in_specs=[pl.BlockSpec(memory_space=pltpu.SMEM), vmem, vmem],
+        in_specs=[pl.BlockSpec(memory_space=pltpu.SMEM), hbm, hbm],
         out_specs=vmem,
         scratch_shapes=[
+            buffer(3, lx, plane, width), buffer(lx, lz, ly), dma((2,)),
             buffer(3, 1, plane, width), buffer(3, 1, plane, width),
             buffer(3, lx, 8, width), buffer(3, lx, 8, width),
             buffer(3, lx * ly, width), buffer(3, lx * ly, width),
             buffer(3, width + 8, cells), buffer(9, width + 8, cells),
-            buffer(3, pairs + 8, cells), buffer(sbuf_rows, LANES),
-            pltpu.VMEM((6 * cells, LANES), jnp.bfloat16),
+            buffer(3, table_rows, cells), pltpu.VMEM((ny * hx * 2 * longest, 6 * cells), jnp.bfloat16),
+            pltpu.VMEM((6 * cells, LANES), jnp.bfloat16), buffer(cells, LANES),
             buffer(cells + 2 * plane, width), buffer(lx, plane + 2 * lz, width), buffer(2, cells + 16, width),
             buffer(2, ny, hx, rows, LANES), buffer(2, ny, hx, rows, LANES),
             buffer(2, ny, hx, rows, LANES), buffer(2, ny, hx, rows, LANES),
             buffer(nx - 1, rows, LANES),
             dma((5,)), dma((5,)),
-        ] + [dma((stages, 2, ny))] * 4 + [dma((stages, nx - 1))] * 2,
+        ] + [dma((stages, 2))] * 2 + [dma((stages, 2, bits))] * 2 + [dma((stages, nx - 1))] * 2,
         compiler_params=pltpu.CompilerParams(
-            collective_id=0, has_side_effects=True, vmem_limit_bytes=48 * 1024 * 1024
+            collective_id=0, has_side_effects=True, vmem_limit_bytes=62 * 1024 * 1024
         ),
-    )(pair_owner, modes.reshape(3, lx, plane, width), cell_weight.reshape(cells, 1))
+    )(pair_owner, modes.reshape(3, lx, plane, width), cell_weight.transpose(0, 2, 1))
 
 
 def solution(mesh):

time: 45.1 us -> 45.5 us (level)
  Pallas kernels: 41.9 us -> 43.8 us
  local copies, waits for them, and re-layouts: 3.01 us -> 1.54 us
    pallas_call x1, Pallas kernels: 41.9 us -> 43.8 us  [shards(): pl.pallas_call(functools.partial(convective_kernel, (nx, ny, nz), (lx, ly...]
    unnamed x6 -> x1, local copies, waits for them, and re-layouts: 2.94 us -> 1.54 us
where the time goes in v4:
time: 45.5 us; the launch traced here: 45.3 us
  Pallas kernels  43.8 us (96%)
  local copies, waits for them, and re-layouts  1.54 us (3%)
    pallas_call x1, Pallas kernels, shards(): pl.pallas_call(functools.partial(convective_kernel, (nx, ny, nz), (lx, ly...  43.8 us
    unnamed x1, local copies, waits for them, and re-layouts  1.54 us

profile of v4, /device:TPU:0, one launch (start us, length us, event | category | flops | bytes accessed | tf_op | source)
XLA Modules:
  0.0 45.3 jit_solution(10148709668005593681)
XLA Ops:
  0.0 43.8 %shard_map.37 = f32[64,258]{1,0:T(8,128)} custom-call(s32[32]{0:T(128)} %owner.1, f32[3,4,32,128]{3,2,1,0:T(8,128)} %bitcast.2, f32[4,4,8]{2,1,0:T(4,128)} %bitcast.3), custom_call_target="tpu_custom_call" | custom-call | tf_op jit(solution)/shard_map/pallas_call | solution.py:255
  43.8 1.5 %copy.5 = f32[64,258]{1,0:T(8,128)} copy(f32[64,258]{1,0:T(8,128)} %shard_map.37) | data formatting | bytes 132096

commit v5 on v4

--- a/solution.py
+++ b/solution.py
@@ -9,7 +9,8 @@
 
 TEST = 64
 LANES = 128
-STAGES = 4
+STAGES = 2
+UNROLL = 4
 
 
 def bounds(rows):
@@ -50,19 +51,21 @@
     for group in range(width // 8):
         tiles = width // 8 - group
 
-        @pl.loop(group * 8, group * 8 + 8)
-        def _(j):
-            start = j * width - (j * (j - 1)) // 2
-            mj = [mt[b, pl.ds(j, 1), :] for b in range(3)]
-            gj = [gt[c, pl.ds(j, 1), :] for c in range(9)]
-            for t in range(tiles):
-                mk = [mt[b, pl.ds(j + 8 * t, 8), :] for b in range(3)]
-                for a in range(3):
-                    terms = [
-                        mj[b] * gt[3 * a + b, pl.ds(j + 8 * t, 8), :] + gj[3 * a + b] * mk[b]
-                        for b in range(3)
-                    ]
-                    hbuf[a, pl.ds(start + 8 * t, 8), :] = terms[0] + terms[1] + terms[2]
+        @pl.loop(0, 8 // UNROLL)
+        def _(step):
+            for ahead in range(UNROLL):
+                j = group * 8 + step * UNROLL + ahead
+                start = j * width - (j * (j - 1)) // 2
+                mj = [mt[b, pl.ds(j, 1), :] for b in range(3)]
+                gj = [gt[c, pl.ds(j, 1), :] for c in range(9)]
+                for t in range(tiles):
+                    mk = [mt[b, pl.ds(j + 8 * t, 8), :] for b in range(3)]
+                    for a in range(3):
+                        terms = [
+                            mj[b] * gt[3 * a + b, pl.ds(j + 8 * t, 8), :] + gj[3 * a + b] * mk[b]
+                            for b in range(3)
+                        ]
+                        hbuf[a, pl.ds(start + 8 * t, 8), :] = terms[0] + terms[1] + terms[2]
 
 
 def split(value):
@@ -211,7 +214,11 @@
                 lines[c, d] = remote(acc.at[to // hx, 0, lax.rem(to, hx), rows], from_gx.at[d - 1, rows],
                                      gx_send.at[c, d - 1], gx_recv.at[c, d - 1], {"gx": to})
 
-    stages = [across_cores, chip_sums] + [functools.partial(across_gy, k=k) for k in range(bits)]
+    def chip(c):
+        across_cores(c)
+        chip_sums(c)
+
+    stages = [chip] + [functools.partial(across_gy, k=k) for k in range(bits)]
     for wave in range(len(parts) + len(stages) - 1):
         for k, stage in enumerate(stages):
             if 0 <= wave - k < len(parts):

time: 45.5 us -> 44 us (0.967)
  Pallas kernels: 43.8 us -> 42.3 us
    pallas_call x1, Pallas kernels: 43.8 us -> 42.3 us  [shards(): pl.pallas_call(functools.partial(convective_kernel, (nx, ny, nz), (lx, ly...]
where the time goes in v5:
time: 44 us; the launch traced here: 43.9 us
  Pallas kernels  42.3 us (96%)
  local copies, waits for them, and re-layouts  1.54 us (4%)
    pallas_call x1, Pallas kernels, shards(): pl.pallas_call(functools.partial(convective_kernel, (nx, ny, nz), (lx, ly...  42.3 us
    unnamed x1, local copies, waits for them, and re-layouts  1.54 us

profile of v5, /device:TPU:0, one launch (start us, length us, event | category | flops | bytes accessed | tf_op | source)
XLA Modules:
  0.0 43.9 jit_solution(11485346634925234723)
XLA Ops:
  0.0 42.3 %shard_map.37 = f32[64,258]{1,0:T(8,128)} custom-call(s32[32]{0:T(128)} %owner.1, f32[3,4,32,128]{3,2,1,0:T(8,128)} %bitcast.2, f32[4,4,8]{2,1,0:T(4,128)} %bitcast.3), custom_call_target="tpu_custom_call" | custom-call | tf_op jit(solution)/shard_map/pallas_call | solution.py:262
  42.3 1.5 %copy.5 = f32[64,258]{1,0:T(8,128)} copy(f32[64,258]{1,0:T(8,128)} %shard_map.37) | data formatting | bytes 132096

commit v6 on v5

--- a/solution.py
+++ b/solution.py
@@ -10,7 +10,8 @@
 TEST = 64
 LANES = 128
 STAGES = 2
-UNROLL = 4
+UNROLL = 2
+CHUNK = 688
 
 
 def bounds(rows):
@@ -78,7 +79,7 @@
 
 
 def convective_kernel(mesh_shape, local_shape, block, scale, owner, m_hbm, cw_hbm, out, m_ref, cw, load,
-                      x_before, x_after, y_before, y_after, z_face, z_out, mt, gt, hbuf, lhs, rhs, wide, ext, eyt, ezt,
+                      x_before, x_after, y_before, y_after, z_face, z_out, mt, gt, hbuf, sbuf, rhs, wide, ext, eyt, ezt,
                       part, acc, from_core, from_gy, from_gx, face_send, face_recv,
                       core_send, core_recv, gy_send, gy_recv, gx_send, gx_recv):
     nx, ny, nz = mesh_shape
@@ -147,35 +148,34 @@
         high, low = split(m[:, :TEST] * weight)
         rhs[pl.ds(a * cells, cells), :] = jnp.concatenate([high, low], axis=1)
         rhs[pl.ds((3 + a) * cells, cells), :] = jnp.concatenate([high, jnp.zeros_like(low)], axis=1)
-    spare = hbuf.shape[1] - pairs
-    for a in range(3):
-        hbuf[a, pl.ds(pairs, spare), :] = jnp.zeros((spare, cells), jnp.float32)
+    spare = sbuf.shape[0] - pairs
+    sbuf[pl.ds(pairs, spare), :] = jnp.zeros((spare, LANES), jnp.float32)
     for copy in arrivals:
         copy.wait_recv()
     transposed_gradients(lx, ly, lz, cz, m_ref, (x_before, x_after, y_before, y_after, z_face), gt, ext, eyt, ezt)
     pair_products(width, mt, gt, hbuf)
 
+    @pl.loop(0, pairs // CHUNK)
+    def _(c):
+        here = pl.ds(pl.multiple_of(c * CHUNK, 16), CHUNK)
+        pieces = [split(hbuf[a, here, :]) for a in range(3)]
+        left = jnp.concatenate([high for high, _ in pieces] + [low for _, low in pieces], axis=1)
+        both = jnp.dot(left, rhs[...], preferred_element_type=jnp.float32)
+        sbuf[here, :] = both + pltpu.roll(both, TEST, 1)
+
     orders = [list(range(bits)), list(reversed(range(bits)))]
     masks = [[sum((r >> (bits - 1 - k) & 1) << b for k, b in enumerate(orders[h])) for r in range(ny)] for h in range(2)]
 
     def products(c, h, level, into):
         rows_from, count = parts[c]
+        first = lax.broadcasted_iota(jnp.int32, (count, LANES), 1) < TEST
         for r in range(ny):
             @pl.loop(0, hx)
             def _(t):
                 slot = ((h * hx + t) * ny + position(masks[h][r])) * nz + level
                 start = owner[slot] * block + rows_from
-                at = pl.ds(pl.multiple_of((r * hx + t) * 2 * count, 16), 2 * count)
-                for a in range(3):
-                    both = [hbuf[a, pl.ds(start, count), :], hbuf[a, pl.ds(start + half, count), :]]
-                    high, low = split(jnp.concatenate(both, axis=0))
-                    lhs[at, pl.ds(a * cells, cells)] = high
-                    lhs[at, pl.ds((3 + a) * cells, cells)] = low
-
-        result = jnp.dot(lhs[pl.ds(0, ny * hx * 2 * count), :], rhs[...], preferred_element_type=jnp.float32)
-        result = (result + pltpu.roll(result, TEST, 1)).reshape(ny, hx, 2, count, LANES)
-        first = lax.broadcasted_iota(jnp.int32, (ny, hx, count, LANES), 3) < TEST
-        into[h, :, :, pl.ds(rows_from, count), :] = jnp.where(first, result[:, :, 0], result[:, :, 1])
+                low, high = sbuf[pl.ds(start, count), :], sbuf[pl.ds(start + half, count), :]
+                into[h, r, t, pl.ds(rows_from, count), :] = jnp.where(first, low, high)
 
     first_hop, hops, lines = {}, {}, {}
 
@@ -250,7 +250,6 @@
     scale = 1.0 / math.sqrt(3.0 * cells * slots)
     table_rows = (slots * block + half + rows + 7) // 8 * 8
     stages = len(bounds(rows))
-    longest = max(count for _, count in bounds(rows))
     bits = ny.bit_length() - 1
     vmem = pl.BlockSpec(memory_space=pltpu.VMEM)
     hbm = pl.BlockSpec(memory_space=pltpu.HBM)
@@ -270,7 +269,7 @@
             buffer(3, lx, 8, width), buffer(3, lx, 8, width),
             buffer(3, lx * ly, width), buffer(3, lx * ly, width),
             buffer(3, width + 8, cells), buffer(9, width + 8, cells),
-            buffer(3, table_rows, cells), pltpu.VMEM((ny * hx * 2 * longest, 6 * cells), jnp.bfloat16),
+            buffer(3, pairs + 8, cells), buffer(table_rows, LANES),
             pltpu.VMEM((6 * cells, LANES), jnp.bfloat16), buffer(cells, LANES),
             buffer(cells + 2 * plane, width), buffer(lx, plane + 2 * lz, width), buffer(2, cells + 16, width),
             buffer(2, ny, hx, rows, LANES), buffer(2, ny, hx, rows, LANES),

time: 44 us -> 43 us (0.977)
  Pallas kernels: 42.3 us -> 41.3 us
    pallas_call x1, Pallas kernels: 42.3 us -> 41.3 us  [shards(): pl.pallas_call(functools.partial(convective_kernel, (nx, ny, nz), (lx, ly...]
where the time goes in v6:
time: 43 us; the launch traced here: 42.9 us
  Pallas kernels  41.3 us (96%)
  local copies, waits for them, and re-layouts  1.54 us (4%)
    pallas_call x1, Pallas kernels, shards(): pl.pallas_call(functools.partial(convective_kernel, (nx, ny, nz), (lx, ly...  41.3 us
    unnamed x1, local copies, waits for them, and re-layouts  1.54 us

profile of v6, /device:TPU:0, one launch (start us, length us, event | category | flops | bytes accessed | tf_op | source)
XLA Modules:
  0.0 42.9 jit_solution(17138399681021692930)
XLA Ops:
  0.0 41.3 %shard_map.37 = f32[64,258]{1,0:T(8,128)} custom-call(s32[32]{0:T(128)} %owner.1, f32[3,4,32,128]{3,2,1,0:T(8,128)} %bitcast.2, f32[4,4,8]{2,1,0:T(4,128)} %bitcast.3), custom_call_target="tpu_custom_call" | custom-call | tf_op jit(solution)/shard_map/pallas_call | solution.py:261
  41.3 1.5 %copy.5 = f32[64,258]{1,0:T(8,128)} copy(f32[64,258]{1,0:T(8,128)} %shard_map.37) | data formatting | bytes 132096
